TPU v7x, 128 devices: a whole 4x4x4 slice. The times are simulated.
128 devices in a mesh: ctx: 16 (over z, y), exp: 8 (over x, core).
Axes of the slice: x: 4, y: 4, z: 4, core: 2. Of those that a mesh axis runs over, the one named last changes fastest.
Arguments:
- attention: bfloat16 [8, 2048, 4096], P('exp', None, 'ctx'), may hold values from -6 to 6
- out_weight: bfloat16 [4096, 2880], P('ctx', 'exp'), may hold values from -0.09375 to 0.09375
- norm_gain: float32 [2880], replicated, may hold values from 0.1 to 1.9
- w_gate: bfloat16 [128, 2880, 1440], P(('ctx', 'exp')), may hold values from -0.109375 to 0.109375
- w_up: bfloat16 [128, 2880, 1440], P(('ctx', 'exp')), may hold values from -0.109375 to 0.109375
- w_down: bfloat16 [128, 1440, 2880], P(('ctx', 'exp')), may hold values from -0.15625 to 0.15625
- routes: int32 [8, 2048, 4], P('exp', 'ctx'), may hold values from 0 to 127, all different within a row; in each aligned block of 128 rows (0 to 127, 128 to 255, ..., all dimensions but the last counted through in order) at most 6 rows name the same one
- gate_fixed: int32 [8, 2048, 4], P('exp', 'ctx'), may hold values from 1 to 65536
Outputs:
- layer_out: bfloat16 [8, 2048, 2880], P('exp', 'ctx')
Inputs may be any that keep to these rules, and one draw needn't show every extreme that they name: `routes`: each token names four different experts. Among the 128 tokens of one device no expert is named by more than 6 tokens, a bound that some block reaches.
All inputs are finite; a program needn't handle non-finite values.
Results may differ from a plain program's by a relative error of at most 0.02.
Values may be sent and summed in bfloat16 or wider, within the bound.
A program may use at most 128 MiB of HBM per device.

v0:
```python
import jax
import jax.numpy as jnp
from jax import lax
from jax.sharding import PartitionSpec as P


def shards(attention, out_weight, norm_gain, w_gate, w_up, w_down, routes, gate_fixed):
    ctx_count = lax.axis_size("ctx")
    exp_count = lax.axis_size("exp")
    device_count = ctx_count * exp_count
    regrouped = lax.all_to_all(attention, "ctx", split_axis=1, concat_axis=2, tiled=True)
    tokens = regrouped[0]
    tok_count = tokens.shape[0]
    width = out_weight.shape[1] * exp_count
    wide_rows = lax.all_gather(out_weight, "exp", axis=1, tiled=True)
    projected = jnp.dot(
        tokens,
        lax.all_gather(wide_rows, "ctx", axis=0, tiled=True),
        preferred_element_type=jnp.float32,
    ).astype(jnp.bfloat16)
    widened = projected.astype(jnp.float32)
    scale_rows = lax.rsqrt(jnp.mean(widened * widened, axis=-1, keepdims=True) + 1e-05)
    normed = (widened * scale_rows * norm_gain).astype(jnp.bfloat16)
    capacity = 6 * tok_count // device_count
    expert_ids = routes[0].reshape(-1)
    pair_count = expert_ids.shape[0]
    token_index = jnp.arange(pair_count, dtype=jnp.int32) // 4
    onehot = (expert_ids[:, None] == jnp.arange(device_count, dtype=jnp.int32)[None, :]).astype(
        jnp.int32
    )
    position = jnp.sum((jnp.cumsum(onehot, axis=0) - onehot) * onehot, axis=1)
    slot_index = expert_ids * capacity + position
    outgoing = (
        jnp.zeros((device_count * capacity, width), jnp.bfloat16)
        .at[slot_index]
        .set(normed[token_index])
    )
    arrived_rows = lax.all_to_all(
        outgoing.reshape(device_count, capacity, width),
        ("ctx", "exp"),
        split_axis=0,
        concat_axis=0,
        tiled=True,
    )
    arrived = arrived_rows.reshape(-1, width)
    gate_value = jnp.dot(arrived, w_gate[0], preferred_element_type=jnp.float32)
    up_value = jnp.dot(arrived, w_up[0], preferred_element_type=jnp.float32)
    activated = (gate_value * jax.nn.sigmoid(1.702 * gate_value) * (up_value + 1.0)).astype(
        jnp.bfloat16
    )
    results = (
        jnp.dot(activated, w_down[0], preferred_element_type=jnp.float32)
        .astype(jnp.bfloat16)
        .reshape(device_count, capacity, width)
    )
    returned = lax.all_to_all(results, ("ctx", "exp"), split_axis=0, concat_axis=0, tiled=True)
    picked = (
        returned.reshape(-1, width)[slot_index].astype(jnp.float32).reshape(tok_count, 4, width)
    )
    weights = gate_fixed[0].astype(jnp.float32) / 65536.0
    combined = jnp.sum(picked * weights[:, :, None], axis=1)
    return (widened + combined).astype(jnp.bfloat16)[None]


def solution(mesh):
    in_specs = (
        P("exp", None, "ctx"),
        P("ctx", "exp"),
        P(),
        P(("ctx", "exp"), None, None),
        P(("ctx", "exp"), None, None),
        P(("ctx", "exp"), None, None),
        P("exp", "ctx", None),
        P("exp", "ctx", None),
    )
    out_specs = P("exp", "ctx", None)
    return jax.shard_map(shards, mesh=mesh, in_specs=in_specs, out_specs=out_specs, check_vma=False)
```

profile of v0, /device:TPU:1, one launch (start us, length us, event | category | flops | bytes accessed | tf_op | source)
XLA Modules:
  0.0 509.3 jit_solution(1411599897944099069)
XLA Ops:
  7.3 29.7 %all-gather.3.cloned.1.call-done = bf16[256,2880]{0,1:T(8,128)(2,1)} async-done(((bf16[256,360]{0,1:T(8,128)(2,1)}), bf16[256,2880]{0,1:T(8,128)(2,1)}) %all-gather.3.cloned.1.call-update) | async-done | bytes 1474576 | tf_op jit(solution)/shard_map/all_gather | solution.py:15
  37.0 3.2 copy.42
  40.7 10.6 %reduce = bf16[2048,256]{1,0:T(8,128)(2,1)S(1)} reduce(bf16[2048,1,256]{2,1,0:T(2,128)(2,1)S(1)} %bitcast.48, bf16[]{:T(256)} %broadcast.145), dimensions={1}, to_apply=%bitcast.43.reduce_sub_computation | reduce | bytes 2097154
  51.3 1.2 reshape.159
  52.5 6.7 %all-to-all-start = ((bf16[16,2,16384]{2,1,0:T(2,128)(2,1)}), bf16[16,2,16384]{2,1,0:T(2,128)(2,1)S(1)}, u32[]{:S(2)}, u32[]{:S(2)}) async-start(bf16[16,2,16384]{2,1,0:T(2,128)(2,1)} %reshape.159), calls=%async_computation | async-start | bytes 2097152 | tf_op jit(solution)/shard_map/all_to_all | solution.py:11
  60.5 23.8 %all-to-all-done = bf16[16,2,16384]{2,1,0:T(2,128)(2,1)S(1)} async-done(((bf16[16,2,16384]{2,1,0:T(2,128)(2,1)}), bf16[16,2,16384]{2,1,0:T(2,128)(2,1)S(1)}, u32[]{:S(2)}, u32[]{:S(2)}) %all-to-all-start) | async-done | bytes 1048608 | tf_op jit(solution)/shard_map/all_to_all | solution.py:11
  86.2 116.8 %all-gather.5.cloned.1.call-done = bf16[4096,2880]{0,1:T(8,128)(2,1)} async-done(((bf16[256,2880]{0,1:T(8,128)(2,1)}), bf16[4096,2880]{0,1:T(8,128)(2,1)}) %all-gather.5.cloned.1.call-update) | async-done | bytes 23592976 | tf_op jit(solution)/shard_map/all_gather | solution.py:18
  203.0 11.4 %multiply_reduce_fusion.1 = (f32[128]{0:T(128)S(1)}, f32[128,2880]{0,1:T(8,128)S(1)}) fusion(bf16[4096,2880]{0,1:T(8,128)(2,1)} %all-gather.5.cloned.1.call-done, bf16[128,4096]{0,1:T(8,128)(2,1)S(1)} %bitcast.51), kind=kOutput, calls=%fused_computation.19 | convolution fusion | flops 3021373440 | bytes 26116608 | tf_op jit(solution)/shard_map/dot_general | solution.py:16
  216.3 16.8 %scatter_custom_fusion = bf16[768,2880]{1,0:T(8,128)(2,1)} fusion(s32[512]{0:T(512)S(1)} %bitcast.55, bf16[128,2880]{1,0:T(8,128)(2,1)S(1)} %copy.36, s32[1024]{0:T(1024)S(1)} %pad_clamp_fusion.1, bf16[]{:T(256)} %constant.17.clone.1), kind=kCustom, calls=%fused_computation.14 | custom fusion | bytes 4423682 | tf_op jit(solution)/shard_map/scatter | solution.py:36
  233.1 7.6 %reshape.124 = bf16[128,6,2880]{2,1,0:T(8,128)(2,1)} reshape(bf16[768,2880]{1,0:T(8,128)(2,1)} %scatter_custom_fusion) | data formatting | bytes 8847360 | tf_op jit(solution)/shard_map/reshape | solution.py:39
  240.7 81.2 %all_to_all.25 = bf16[128,6,2880]{2,1,0:T(8,128)(2,1)} all-to-all(bf16[128,6,2880]{2,1,0:T(8,128)(2,1)} %reshape.124), channel_id=1, replica_groups=mesh['ctx'=16,'exp'=8] {'ctx','exp'}, dimensions={0} | all-to-all | bytes 8847360 | tf_op jit(solution)/shard_map/all_to_all | solution.py:38
  321.9 8.2 %reshape.125 = bf16[768,2880]{1,0:T(8,128)(2,1)} reshape(bf16[128,6,2880]{2,1,0:T(8,128)(2,1)} %all_to_all.25) | data formatting | bytes 8847360 | tf_op jit(solution)/shard_map/reshape | solution.py:45
  330.0 12.3 %fusion.2 = f32[768,1440]{0,1:T(8,128)} fusion(bf16[768,2880]{1,0:T(8,128)(2,1)} %reshape.125, bf16[1,2880,1440]{1,2,0:T(8,128)(2,1)} %param.12), kind=kOutput, calls=%fused_computation.5 | convolution fusion | flops 6370099200 | bytes 17141760 | tf_op jit(solution)/shard_map/dot_general | solution.py:47
  342.3 36.0 %fusion.6 = bf16[768,2880]{0,1:T(8,128)(2,1)} fusion(bf16[1,1440,2880]{2,1,0:T(8,128)(2,1)} %param.13, f32[768,1440]{0,1:T(8,128)} %fusion.2, bf16[768,2880]{1,0:T(8,128)(2,1)} %reshape.125, bf16[1,2880,1440]{1,2,0:T(8,128)(2,1)} %param.11), kind=kOutput, calls=%fused_computation.10 | convolution fusion | flops 12751257600 | bytes 29859840 | tf_op jit(solution)/shard_map/dot_general | solution.py:52
  378.3 6.5 %copy.37 = bf16[768,2880]{1,0:T(8,128)(2,1)} copy(bf16[768,2880]{0,1:T(8,128)(2,1)} %fusion.6) | data formatting | bytes 8847360 | tf_op jit(solution)/shard_map/convert_element_type | solution.py:53
  384.8 7.6 %reshape.126 = bf16[128,6,2880]{2,1,0:T(8,128)(2,1)} reshape(bf16[768,2880]{1,0:T(8,128)(2,1)} %copy.37) | data formatting | bytes 8847360 | tf_op jit(solution)/shard_map/reshape | solution.py:54
  392.4 5.9 %all-to-all-start.2 = ((bf16[128,6,2880]{2,1,0:T(8,128)(2,1)}), bf16[128,6,2880]{2,1,0:T(8,128)(2,1)}, u32[]{:S(2)}, u32[]{:S(2)}) async-start(bf16[128,6,2880]{2,1,0:T(8,128)(2,1)} %reshape.126), calls=%async_computation.2 | async-start | bytes 12058624 | tf_op jit(solution)/shard_map/all_to_all | solution.py:56
  398.4 72.3 %all-to-all-done.2 = bf16[128,6,2880]{2,1,0:T(8,128)(2,1)} async-done(((bf16[128,6,2880]{2,1,0:T(8,128)(2,1)}), bf16[128,6,2880]{2,1,0:T(8,128)(2,1)}, u32[]{:S(2)}, u32[]{:S(2)}) %all-to-all-start.2) | async-done | bytes 4423712 | tf_op jit(solution)/shard_map/all_to_all | solution.py:56
  470.7 8.2 %reshape.127 = bf16[768,2880]{1,0:T(8,128)(2,1)} reshape(bf16[128,6,2880]{2,1,0:T(8,128)(2,1)} %all-to-all-done.2) | data formatting | bytes 8847360 | tf_op jit(solution)/shard_map/reshape | solution.py:58
  478.9 8.7 %gather_fusion = bf16[512,2880]{1,0:T(8,128)(2,1)S(1)} fusion(bf16[768,2880]{1,0:T(8,128)(2,1)} %reshape.127, s32[1024]{0:T(1024)S(1)} %pad_clamp_fusion), kind=kCustom, calls=%fused_computation.1 | custom fusion | bytes 5900288 | tf_op jit(solution)/shard_map/gather | solution.py:58
  487.6 3.6 reshape.128
  491.2 7.1 %multiply_reduce_fusion = f32[128,2880]{1,0:T(8,128)S(1)} fusion(f32[128,4,2880]{2,1,0:T(4,128)} %reshape.128, f32[128,4]{1,0:T(8,128)S(1)} %copy.38), kind=kLoop, calls=%fused_computation.9 | loop fusion | flops 2580480 | bytes 7374848 | tf_op jit(solution)/shard_map/reduce_sum | solution.py:61
  498.3 1.6 copy.39
  499.9 2.4 fusion.15
  (42 shorter events, 6.4 us)
Async XLA Ops:
  6.5 30.5 %all-gather.3.cloned.1.call-start = ((), (), s32[]{:S(2)}) async-start(), calls=%async_computation.3 | async-start | bytes 1658880 | tf_op jit(solution)/shard_map/all_gather | solution.py:15
  7.3 195.7 %all-gather.5.cloned.1.call-start = ((), (), s32[]{:S(2)}) async-start(), calls=%async_computation.4 | async-start | bytes 25067520 | tf_op jit(solution)/shard_map/all_gather | solution.py:18
  40.2 19.0 %copy-start.3 = (s32[1,128,4]{1,2,0:T(4,128)S(1)}, s32[1,128,4]{1,2,0:T(4,128)}, u32[]{:S(2)}) copy-start(s32[1,128,4]{1,2,0:T(4,128)} %param.14) | copy-start | bytes 6148
  52.5 31.8 %all-to-all-start = ((bf16[16,2,16384]{2,1,0:T(2,128)(2,1)}), bf16[16,2,16384]{2,1,0:T(2,128)(2,1)S(1)}, u32[]{:S(2)}, u32[]{:S(2)}) async-start(bf16[16,2,16384]{2,1,0:T(2,128)(2,1)} %reshape.159), calls=%async_computation | async-start | bytes 2097152 | tf_op jit(solution)/shard_map/all_to_all | solution.py:11
  203.0 12.6 %copy-start.2 = (f32[2880]{0:T(1024)S(1)}, f32[2880]{0:T(1024)}, u32[]{:S(2)}) copy-start(f32[2880]{0:T(1024)} %param.10) | copy-start | bytes 34564
  214.4 1.1 copy-start
  392.4 5.9 %copy-start.4 = (s32[1,128,4]{1,2,0:T(4,128)S(1)}, s32[1,128,4]{1,2,0:T(4,128)}, u32[]{:S(2)}) copy-start(s32[1,128,4]{1,2,0:T(4,128)} %param.15) | copy-start | bytes 6148
  392.4 78.4 %all-to-all-start.2 = ((bf16[128,6,2880]{2,1,0:T(8,128)(2,1)}), bf16[128,6,2880]{2,1,0:T(8,128)(2,1)}, u32[]{:S(2)}, u32[]{:S(2)}) async-start(bf16[128,6,2880]{2,1,0:T(8,128)(2,1)} %reshape.126), calls=%async_computation.2 | async-start | bytes 12058624 | tf_op jit(solution)/shard_map/all_to_all | solution.py:56
  491.2 8.7 %copy-start.1 = (f32[128,2880]{0,1:T(8,128)S(1)}, f32[128,2880]{0,1:T(8,128)}, u32[]{:S(2)}) copy-start(f32[128,2880]{0,1:T(8,128)} %copy-done) | copy-start | bytes 4423684
Sparse Core Ops, SparseCore 0:
  9.0 27.9 all-gather.2
  39.1 163.8 all-gather.4
where the time goes:
time: 516 us; the launch traced here: 509 us
  waiting for transfers between devices  243 us (47%)
  blocking collectives  81.2 us (16%)
  local copies, waits for them, and re-layouts  77.7 us (15%)
  matrix products  59.6 us (12%)
  other arithmetic  21.1 us (4%)
  between operations  13.8 us (3%)
  starting transfers between devices  12.7 us (2%)
    all_gather x1, waiting for transfers between devices, shards(): lax.all_gather(wide_rows, 'ctx', axis=0, tiled=True)  117 us
    all_to_all x1, blocking collectives, shards(): lax.all_to_all(outgoing.reshape(device_count, capacity, width), ('ctx', '...  81.2 us
    all_to_all x1, waiting for transfers between devices, shards(): lax.all_to_all(results, ('ctx', 'exp'), split_axis=0, concat_axis=0, tile...  72.3 us
    dot_general x1, matrix products, shards(): jnp.dot(activated, w_down[0], preferred_element_type=jnp.float32)  36 us
    all_gather x1, waiting for transfers between devices, shards(): wide_rows = lax.all_gather(out_weight, 'exp', axis=1, tiled=True)  29.7 us
    all_to_all x1, waiting for transfers between devices, shards(): lax.all_to_all(attention, 'ctx', split_axis=1, concat_axis=2, tiled=True)  23.8 us
    scatter x1, local copies, waits for them, and re-layouts, shards(): outgoing = jnp.zeros((device_count * capacity, width), jnp.bfloat16).at[s...  16.8 us
    dot_general x1, matrix products, shards(): up_value = jnp.dot(arrived, w_up[0], preferred_element_type=jnp.float32)  12.3 us
  transfers between devices with their start and end apart: 4, of which 4 were waited for; matrix products, arithmetic and copies ran while one was open for 4% of the time, Pallas kernels for 0%

commit v1 on v0

v1 whole, which is shorter than its diff:
```python
import functools

import jax
import jax.numpy as jnp
from jax import lax
from jax.experimental import pallas as pl
from jax.experimental.pallas import tpu as pltpu
from jax.sharding import PartitionSpec as P

MESH = pl.DeviceIdType.MESH
BF16, F32, I32 = jnp.bfloat16, jnp.float32, jnp.int32

D = 2880
FFW = 1440
TOK = 128
CAP = 6
DEV = 128
SLICE = 384
PIECES = 8
WIDE = SLICE * PIECES
ROWS = PIECES * CAP
BLOCK = 8
BROWS = BLOCK * CAP
GROUP = 32
GROUPS = DEV // GROUP
GROWS = GROUP * CAP
VMEM = 56 * 1024 * 1024


def offsets(slot):
    group, rest = slot // GROUP, slot % GROUP
    dz, dy, dc = rest // 8, (rest // 2) % 4, rest % 2
    return dz, dy, (group + 8 - dz - dy) % 4, dc


def partner(slot, back):
    ctx, exp = lax.axis_index("ctx"), lax.axis_index("exp")
    dz, dy, dx, dc = offsets(slot)
    if back:
        dz, dy, dx = 4 - dz, 4 - dy, 4 - dx
    z, y = (ctx // 4 + dz) % 4, (ctx % 4 + dy) % 4
    x, core = (exp // 2 + dx) % 4, (exp % 2 + dc) % 2
    return z * 4 + y, x * 2 + core


def unpack(mixer, messages):
    flat = messages.reshape(BLOCK * ROWS, SLICE)
    sorted_rows = jnp.dot(mixer, flat, preferred_element_type=F32).astype(BF16)
    return [sorted_rows[piece * BROWS : (piece + 1) * BROWS] for piece in range(PIECES)]


def pack(mixer_t, rows):
    stacked = jnp.concatenate(
        [rows[:, piece * SLICE : (piece + 1) * SLICE] for piece in range(PIECES)], axis=0
    )
    mixed = jnp.dot(mixer_t, stacked, preferred_element_type=F32).astype(BF16)
    return mixed.reshape(BLOCK, ROWS, SLICE)


def mixers():
    count = BLOCK * ROWS
    place = jnp.arange(count, dtype=I32)
    piece, position, message = place // BROWS, (place // BLOCK) % CAP, place % BLOCK
    source = message * ROWS + piece * CAP + position
    mixer = (source[:, None] == place[None, :]).astype(BF16)
    mixer_t = (place[:, None] == source[None, :]).astype(BF16)
    return mixer, mixer_t


def slot_columns():
    column = jnp.arange(DEV * CAP, dtype=I32)
    block, position, message = column // BROWS, (column // BLOCK) % CAP, column % BLOCK
    ctx, exp = partner(block * BLOCK + message, False)
    return (ctx * 8 + exp).reshape(1, -1).astype(I32), position.reshape(1, -1)


def slot_mask(routes, expert_col, position_col):
    named = [(routes[:, k : k + 1] == expert_col) for k in range(4)]
    chosen = named[0] | named[1] | named[2] | named[3]
    earlier = lax.broadcasted_iota(I32, (TOK, TOK), 1) < lax.broadcasted_iota(I32, (TOK, TOK), 0)
    rank = jnp.dot(
        jnp.where(earlier, 1.0, 0.0).astype(BF16),
        jnp.where(chosen, 1.0, 0.0).astype(BF16),
        preferred_element_type=F32,
    )
    return named, chosen & (rank == position_col.astype(F32))


def dispatch_kernel(projected, gain, routes, expert_col, position_col, mixer_t, send, normed, rows):
    widened = projected[...].astype(F32)
    scale = lax.rsqrt(jnp.mean(widened * widened, axis=-1, keepdims=True) + 1e-05)
    normed[:, D:] = jnp.zeros((TOK, WIDE - D), BF16)
    normed[:, :D] = (widened * scale * gain[...]).astype(BF16)
    _, mask = slot_mask(routes[...], expert_col[...], position_col[...])
    chooser = jnp.transpose(jnp.where(mask, 1.0, 0.0)).astype(BF16)

    @pl.loop(0, PIECES)
    def _(piece):
        columns = pl.ds(pl.multiple_of(piece * SLICE, SLICE), SLICE)
        rows[:, columns] = jnp.dot(
            chooser, normed[:, columns], preferred_element_type=F32
        ).astype(BF16)

    @pl.loop(0, DEV // BLOCK)
    def _(block):
        here = pl.ds(pl.multiple_of(block * BROWS, BROWS), BROWS)
        send[pl.ds(block * BLOCK, BLOCK)] = pack(mixer_t[...], rows[here, :])


def combine_kernel(
    returned, projected, routes, gate_fixed, expert_col, position_col, mixer, out, rows
):
    @pl.loop(0, DEV // BLOCK)
    def _(block):
        here = pl.ds(pl.multiple_of(block * BROWS, BROWS), BROWS)
        pieces = unpack(mixer[...], returned[pl.ds(block * BLOCK, BLOCK)])
        for piece in range(PIECES):
            rows[here, piece * SLICE : (piece + 1) * SLICE] = pieces[piece]

    named, mask = slot_mask(routes[...], expert_col[...], position_col[...])
    fixed = jnp.zeros((TOK, DEV * CAP), I32)
    for k in range(4):
        fixed = fixed + jnp.where(named[k], gate_fixed[:, k : k + 1], 0)
    fixed = jnp.where(mask, fixed, 0)
    high = (fixed // 256).astype(F32).astype(BF16)
    low = (fixed % 256).astype(F32).astype(BF16)
    weights = jnp.concatenate([high, low], axis=0)
    for start in range(0, D, SLICE):
        stop = min(start + SLICE, D)
        total = jnp.dot(weights, rows[:, start:stop], preferred_element_type=F32)
        combined = total[:TOK] * (1.0 / 256.0) + total[TOK:] * (1.0 / 65536.0)
        out[:, start:stop] = (projected[:, start:stop].astype(F32) + combined).astype(BF16)


def expert_kernel(
    send, w_gate, w_up, w_down, mixer, mixer_t,
    returned,
    gate, up, down, landed, results, arrived, activated, outputs,
    weight_sems, send_sem, land_sems, result_sem, return_sem,
):
    loads = [
        pltpu.make_async_copy(source.at[0], target, weight_sems.at[i])
        for i, (source, target) in enumerate(((w_gate, gate), (w_up, up), (w_down, down)))
    ]
    for load in loads:
        load.start()
    barrier = pltpu.get_barrier_semaphore()

    @pl.loop(1, DEV)
    def _(slot):
        pl.semaphore_signal(barrier, inc=1, device_id=partner(slot, False), device_id_type=MESH)

    pl.semaphore_wait(barrier, DEV - 1)
    own = pltpu.make_async_copy(send.at[0], landed.at[0], land_sems.at[0])
    own.start()

    @pl.loop(1, DEV)
    def _(slot):
        pltpu.make_async_remote_copy(
            src_ref=send.at[slot],
            dst_ref=landed.at[slot],
            send_sem=send_sem,
            recv_sem=land_sems.at[slot // GROUP],
            device_id=partner(slot, False),
            device_id_type=MESH,
        ).start()

    outputs[:, D:] = jnp.zeros((GROWS, WIDE - D), BF16)
    for load in loads:
        load.wait()

    @pl.loop(0, GROUPS)
    def _(group):
        first = group * GROUP
        span = landed.at[pl.ds(first, GROUP)]
        pltpu.make_async_copy(span, span, land_sems.at[group]).wait()

        @pl.loop(0, GROUP // BLOCK)
        def _(block):
            here = pl.ds(pl.multiple_of(block * BROWS, BROWS), BROWS)
            pieces = unpack(mixer[...], landed[pl.ds(first + block * BLOCK, BLOCK)])
            for piece in range(PIECES):
                arrived[here, piece * SLICE : (piece + 1) * SLICE] = pieces[piece]

        def hidden(columns):
            gate_value = jnp.dot(arrived[:, :D], gate[:, columns], preferred_element_type=F32)
            up_value = jnp.dot(arrived[:, :D], up[:, columns], preferred_element_type=F32)
            activated[:, columns] = (
                gate_value / (1.0 + jnp.exp(-1.702 * gate_value)) * (up_value + 1.0)
            ).astype(BF16)

        @pl.loop(0, FFW // 256)
        def _(tile):
            hidden(pl.ds(pl.multiple_of(tile * 256, 256), 256))

        hidden(pl.ds(FFW // 256 * 256, FFW % 256))

        def projected_down(columns):
            outputs[:, columns] = jnp.dot(
                activated[...], down[:, columns], preferred_element_type=F32
            ).astype(BF16)

        @pl.loop(0, D // 256)
        def _(tile):
            projected_down(pl.ds(pl.multiple_of(tile * 256, 256), 256))

        projected_down(pl.ds(D // 256 * 256, D % 256))

        @pl.loop(0, GROUP // BLOCK)
        def _(block):
            here = pl.ds(pl.multiple_of(block * BROWS, BROWS), BROWS)
            results[pl.ds(first + block * BLOCK, BLOCK)] = pack(mixer_t[...], outputs[here, :])

        @pl.when(group == 0)
        def _():
            pltpu.make_async_copy(results.at[0], returned.at[0], return_sem).start()

        @pl.loop(jnp.maximum(first, 1), first + GROUP)
        def _(slot):
            pltpu.make_async_remote_copy(
                src_ref=results.at[slot],
                dst_ref=returned.at[slot],
                send_sem=result_sem,
                recv_sem=return_sem,
                device_id=partner(slot, True),
                device_id_type=MESH,
            ).start()

    sent = send.at[pl.ds(1, DEV - 1)]
    pltpu.make_async_copy(sent, sent, send_sem).wait()
    sent = results.at[pl.ds(1, DEV - 1)]
    pltpu.make_async_copy(sent, sent, result_sem).wait()
    pltpu.make_async_copy(returned, returned, return_sem).wait()


def whole(count):
    return [pl.BlockSpec(memory_space=pltpu.VMEM)] * count


def project(attention, out_weight):
    along_z = [[y, 4 + y, 8 + y, 12 + y] for y in range(4)]
    along_y = [[4 * z, 4 * z + 1, 4 * z + 2, 4 * z + 3] for z in range(4)]
    tokens = lax.all_to_all(
        attention[0], "ctx", split_axis=0, concat_axis=1, tiled=True, axis_index_groups=along_z
    )
    weight = lax.all_gather(out_weight, "exp", axis=1, tiled=True)
    weight = lax.all_gather(weight, "ctx", axis=0, tiled=True, axis_index_groups=along_z)
    partial = jnp.dot(tokens, weight, preferred_element_type=F32).astype(BF16)
    parts = lax.all_to_all(
        partial.reshape(4, TOK, D), "ctx", split_axis=0, concat_axis=0, tiled=True,
        axis_index_groups=along_y,
    )
    return jnp.sum(parts.astype(F32), axis=0).astype(BF16)


def shards(attention, out_weight, norm_gain, w_gate, w_up, w_down, routes, gate_fixed):
    mixer, mixer_t = mixers()
    expert_col, position_col = slot_columns()
    projected = project(attention, out_weight)
    message = jax.ShapeDtypeStruct((DEV, ROWS, SLICE), BF16)
    params = pltpu.CompilerParams(vmem_limit_bytes=VMEM)
    send = pl.pallas_call(
        dispatch_kernel,
        out_shape=message,
        in_specs=whole(6),
        out_specs=whole(1)[0],
        scratch_shapes=[pltpu.VMEM((TOK, WIDE), BF16), pltpu.VMEM((DEV * CAP, WIDE), BF16)],
        compiler_params=params,
    )(projected, norm_gain.reshape(1, D), routes[0], expert_col, position_col, mixer_t)
    anywhere = pl.BlockSpec(memory_space=pl.ANY)
    returned = pl.pallas_call(
        expert_kernel,
        out_shape=message,
        in_specs=[anywhere] * 4 + whole(2),
        out_specs=anywhere,
        scratch_shapes=[
            pltpu.VMEM((D, FFW), BF16),
            pltpu.VMEM((D, FFW), BF16),
            pltpu.VMEM((FFW, D), BF16),
            pltpu.VMEM((DEV, ROWS, SLICE), BF16),
            pltpu.VMEM((DEV, ROWS, SLICE), BF16),
            pltpu.VMEM((GROWS, WIDE), BF16),
            pltpu.VMEM((GROWS, FFW), BF16),
            pltpu.VMEM((GROWS, WIDE), BF16),
            pltpu.SemaphoreType.DMA((3,)),
            pltpu.SemaphoreType.DMA,
            pltpu.SemaphoreType.DMA((GROUPS,)),
            pltpu.SemaphoreType.DMA,
            pltpu.SemaphoreType.DMA,
        ],
        compiler_params=pltpu.CompilerParams(
            vmem_limit_bytes=VMEM, collective_id=0, has_side_effects=True
        ),
    )(send, w_gate, w_up, w_down, mixer, mixer_t)
    out = pl.pallas_call(
        combine_kernel,
        out_shape=jax.ShapeDtypeStruct((TOK, D), BF16),
        in_specs=whole(7),
        out_specs=whole(1)[0],
        scratch_shapes=[pltpu.VMEM((DEV * CAP, WIDE), BF16)],
        compiler_params=params,
    )(returned, projected, routes[0], gate_fixed[0], expert_col, position_col, mixer)
    return out[None]


def solution(mesh):
    in_specs = (
        P("exp", None, "ctx"),
        P("ctx", "exp"),
        P(),
        P(("ctx", "exp"), None, None),
        P(("ctx", "exp"), None, None),
        P(("ctx", "exp"), None, None),
        P("exp", "ctx", None),
        P("exp", "ctx", None),
    )
    out_specs = P("exp", "ctx", None)
    return jax.shard_map(shards, mesh=mesh, in_specs=in_specs, out_specs=out_specs, check_vma=False)
```

time: 516 us -> 335 us (0.65); the launches traced: 509 us -> 334 us
  Pallas kernels: 0 us -> 167 us
  waiting for transfers between devices: 243 us -> 86.3 us
  blocking collectives: 81.2 us -> 20.7 us
  matrix products: 59.6 us -> 6.09 us
  local copies, waits for them, and re-layouts: 77.7 us -> 32.8 us
  other arithmetic: 21.1 us -> 3.17 us
  starting transfers between devices: 12.7 us -> 4.04 us
    pallas_call x0 -> x3, Pallas kernels: none -> 167 us  [the longest x1 144 us: shards(): pl.pallas_call(expert_kernel, out_shape=message, in_specs=[anywhere] * 4...]
    all_to_all x2 -> x1, waiting for transfers between devices: 96 us -> 6.59 us  [project(): lax.all_to_all(partial.reshape(4, TOK, D), 'ctx', split_axis=0, concat_ax...]
    all_gather x2, waiting for transfers between devices: 146 us -> 79 us  [the longest x1 49.3 us: project(): lax.all_gather(weight, 'ctx', axis=0, tiled=True, axis_index_groups=along_z)]
    all_to_all x1, blocking collectives: 81.2 us -> 20.7 us  [project(): lax.all_to_all(attention[0], 'ctx', split_axis=0, concat_axis=1, tiled=Tr...]
    dot_general x3 -> x1, matrix products: 59.6 us -> 6.09 us  [project(): partial = jnp.dot(tokens, weight, preferred_element_type=F32).astype(BF16)]
    reshape x4 -> x2, local copies, waits for them, and re-layouts: 31.5 us -> 2.69 us  [the longest x1 2.08 us: project(): partial.reshape(4, TOK, D)]
    unnamed x17 -> x10, local copies, waits for them, and re-layouts: 7.33 us -> 25.1 us
    scatter x1 -> x0, local copies, waits for them, and re-layouts: 16.8 us -> none  [shards(): outgoing = jnp.zeros((device_count * capacity, width), jnp.bfloat16).at[s...]
  transfers between devices with their start and end apart: 4 -> 3, of which waited for: 4 -> 3; matrix products, arithmetic and copies ran while one was open for 4% -> 8% of each run, Pallas kernels for 0% -> 0%
where the time goes in v1:
time: 335 us; the launch traced here: 334 us
  Pallas kernels  167 us (50%)
  waiting for transfers between devices  86.3 us (26%)
  local copies, waits for them, and re-layouts  32.8 us (10%)
  blocking collectives  20.7 us (6%)
  between operations  13.4 us (4%)
  matrix products  6.09 us (2%)
  starting transfers between devices  4.04 us (1%)
    pallas_call x1, Pallas kernels, shards(): pl.pallas_call(expert_kernel, out_shape=message, in_specs=[anywhere] * 4...  144 us
    all_gather x1, waiting for transfers between devices, project(): lax.all_gather(weight, 'ctx', axis=0, tiled=True, axis_index_groups=along_z)  49.3 us
    all_gather x1, waiting for transfers between devices, project(): weight = lax.all_gather(out_weight, 'exp', axis=1, tiled=True)  29.7 us
    unnamed x10, local copies, waits for them, and re-layouts  25.1 us
    all_to_all x1, blocking collectives, project(): lax.all_to_all(attention[0], 'ctx', split_axis=0, concat_axis=1, tiled=Tr...  20.7 us
    pallas_call x1, Pallas kernels, shards(): pl.pallas_call(dispatch_kernel, out_shape=message, in_specs=whole(6), out...  11.9 us
    pallas_call x1, Pallas kernels, shards(): pl.pallas_call(combine_kernel, out_shape=jax.ShapeDtypeStruct((TOK, D), B...  11.3 us
  transfers between devices with their start and end apart: 3, of which 3 were waited for; matrix products, arithmetic and copies ran while one was open for 8% of the time, Pallas kernels for 0%

profile of v1, /device:TPU:1, one launch (start us, length us, event | category | flops | bytes accessed | tf_op | source)
XLA Modules:
  0.0 333.9 jit_solution(11598490218542206125)
XLA Ops:
  6.5 0.7 all-gather.3.cloned.1.call-update
  7.3 0.0 all-gather.5.cloned.1.call-start
  7.3 29.7 %all-gather.3.cloned.1.call-done = bf16[256,2880]{0,1:T(8,128)(2,1)} async-done(((bf16[256,360]{0,1:T(8,128)(2,1)}), bf16[256,2880]{0,1:T(8,128)(2,1)}) %all-gather.3.cloned.1.call-update) | async-done | bytes 1474576 | tf_op jit(solution)/shard_map/all_gather | solution.py:246
  37.0 0.0 all-gather.5.cloned.1.call-update
  37.0 20.7 %all_to_all.24 = bf16[4,512,256]{2,1,0:T(8,128)(2,1)S(1)} all-to-all(bf16[4,512,256]{2,1,0:T(8,128)(2,1)} %bitcast.16), channel_id=1, replica_groups={{0,32,64,96},{8,40,72,104},{16,48,80,112},{24,56,88,120},{1,33,65,97},{..., dimensions={0} | all-to-all | bytes 2097152 | tf_op jit(solution)/shard_map/all_to_all | solution.py:243
  57.8 0.5 copy.25
  58.3 49.3 %all-gather.5.cloned.1.call-done = bf16[1024,2880]{0,1:T(8,128)(2,1)} async-done(((bf16[256,2880]{0,1:T(8,128)(2,1)}), bf16[1024,2880]{0,1:T(8,128)(2,1)}) %all-gather.5.cloned.1.call-update) | async-done | bytes 5898256 | tf_op jit(solution)/shard_map/all_gather | solution.py:247
  107.6 6.1 %fusion = bf16[360,4,8,128]{3,2,1,0:T(8,128)(2,1)S(1)} fusion(bf16[1024,2880]{0,1:T(8,128)(2,1)} %all-gather.5.cloned.1.call-done, bf16[512,1024]{0,1:T(8,128)(2,1)S(1)} %bitcast.17), kind=kOutput, calls=%fused_computation.2 | convolution fusion | flops 3021373440 | bytes 9895936 | tf_op jit(solution)/shard_map/dot_general | solution.py:248
  113.7 2.1 copy.38
  115.8 4.0 %all-to-all-start.1 = ((bf16[4,128,2880]{1,2,0:T(8,128)(2,1)}), bf16[4,128,2880]{1,2,0:T(8,128)(2,1)S(1)}, u32[]{:S(2)}, u32[]{:S(2)}) async-start(bf16[4,128,2880]{1,2,0:T(8,128)(2,1)} %bitcast.13), calls=%async_computation.1 | async-start | bytes 5898240 | tf_op jit(solution)/shard_map/all_to_all | solution.py:249
  119.8 0.7 copy.28
  120.6 0.6 reshape.582.gain
  121.2 11.7 %copy.30.w_gate = bf16[1,2880,1440]{2,1,0:T(8,128)(2,1)} copy(bf16[1,2880,1440]{1,2,0:T(8,128)(2,1)} %param.11) | data formatting | bytes 16588800 | tf_op args[3]
  132.9 11.8 %copy.31.w_up = bf16[1,2880,1440]{2,1,0:T(8,128)(2,1)} copy(bf16[1,2880,1440]{1,2,0:T(8,128)(2,1)} %param.12) | data formatting | bytes 16588800 | tf_op args[4]
  144.7 0.7 copy.32
  145.5 0.7 and_select_fusion
  146.2 0.9 fusion.2
  147.2 6.6 %all-to-all-done.1 = bf16[4,128,2880]{1,2,0:T(8,128)(2,1)S(1)} async-done(((bf16[4,128,2880]{1,2,0:T(8,128)(2,1)}), bf16[4,128,2880]{1,2,0:T(8,128)(2,1)S(1)}, u32[]{:S(2)}, u32[]{:S(2)}) %all-to-all-start.1) | async-done | bytes 2949152 | tf_op jit(solution)/shard_map/all_to_all | solution.py:249
  153.8 1.5 reduce_sum.12
  155.2 2.3 copy.29.projected
  157.5 11.9 %shard_map.82.send = bf16[128,48,384]{2,1,0:T(8,128)(2,1)} custom-call(bf16[128,2880]{1,0:T(8,128)(2,1)} %copy.29.projected, f32[1,2880]{1,0:T(1,128)} %reshape.582.gain, s32[128,4]{1,0:T(8,128)} %bitcast.18, s32[1,768]{1,0:T(1,128)} %get-tuple-element.8.expert_col, s32[1,768]{1,0:T(1,128)} %get-tuple-element.7.position_col, ...), custom_call_target="tpu_custom_call" | custom-call | tf_op jit(solution)/shard_map/pallas_call | solution.py:262
  169.5 144.0 %shard_map.83.returned = bf16[128,48,384]{2,1,0:T(8,128)(2,1)} custom-call(bf16[128,48,384]{2,1,0:T(8,128)(2,1)} %shard_map.82.send, bf16[1,2880,1440]{2,1,0:T(8,128)(2,1)} %copy.30.w_gate, bf16[1,2880,1440]{2,1,0:T(8,128)(2,1)} %copy.31.w_up, bf16[1,1440,2880]{2,1,0:T(8,128)(2,1)} %w_down.1, bf16[384,384]{1,0:T(8,128)(2,1)} %get-tuple-element.5.mixer, ...), custom_call_target="tpu_custom_call" | custom-call | tf_op jit(solution)/shard_map/pallas_call | solution.py:271
  313.5 11.3 %shard_map.84 = bf16[128,2880]{1,0:T(8,128)(2,1)} custom-call(bf16[128,48,384]{2,1,0:T(8,128)(2,1)} %shard_map.83.returned, bf16[128,2880]{1,0:T(8,128)(2,1)} %copy.29.projected, s32[128,4]{1,0:T(8,128)} %bitcast.19, s32[128,4]{1,0:T(8,128)} %bitcast.20, s32[1,768]{1,0:T(1,128)} %get-tuple-element.8.expert_col, s32[1,768]{1,0:T(1,128)} %get-tuple-element.7.position_col, ...), custom_call_target="tpu_custom_call" | custom-call | tf_op jit(solution)/shard_map/pallas_call | solution.py:295
  324.8 2.3 copy.34
  (8 shorter events, 0.0 us)
Async XLA Ops:
  6.5 30.5 %all-gather.3.cloned.1.call-start = ((), (), s32[]{:S(2)}) async-start(), calls=%async_computation.2 | async-start | bytes 1658880 | tf_op jit(solution)/shard_map/all_gather | solution.py:246
  7.3 100.3 %all-gather.5.cloned.1.call-start = ((), (), s32[]{:S(2)}) async-start(), calls=%async_computation.3 | async-start | bytes 7372800 | tf_op jit(solution)/shard_map/all_gather | solution.py:247
  113.7 6.1 %copy-start.1 = (s32[1,128,4]{1,2,0:T(4,128)S(1)}, s32[1,128,4]{1,2,0:T(4,128)}, u32[]{:S(2)}) copy-start(s32[1,128,4]{1,2,0:T(4,128)} %param.14) | copy-start | bytes 6148
  113.7 6.8 %copy-start = (f32[2880]{0:T(1024)S(1)}, f32[2880]{0:T(1024)}, u32[]{:S(2)}) copy-start(f32[2880]{0:T(1024)} %param.10) | copy-start | bytes 34564
  115.8 38.0 %all-to-all-start.1 = ((bf16[4,128,2880]{1,2,0:T(8,128)(2,1)}), bf16[4,128,2880]{1,2,0:T(8,128)(2,1)S(1)}, u32[]{:S(2)}, u32[]{:S(2)}) async-start(bf16[4,128,2880]{1,2,0:T(8,128)(2,1)} %bitcast.13), calls=%async_computation.1 | async-start | bytes 5898240 | tf_op jit(solution)/shard_map/all_to_all | solution.py:249
  132.9 11.9 %copy-start.2 = (s32[1,128,4]{1,2,0:T(4,128)S(1)}, s32[1,128,4]{1,2,0:T(4,128)}, u32[]{:S(2)}) copy-start(s32[1,128,4]{1,2,0:T(4,128)} %param.15) | copy-start | bytes 6148
Sparse Core Ops, SparseCore 0:
  9.0 27.9 all-gather.2
  38.7 68.8 all-gather.4

commit v2 on v0

v2 whole, which is shorter than its diff:
```python
import jax
import jax.numpy as jnp
from jax import lax
from jax.experimental import pallas as pl
from jax.experimental.pallas import tpu as pltpu
from jax.sharding import PartitionSpec as P

MESH = pl.DeviceIdType.MESH
BF16, F32, I32 = jnp.bfloat16, jnp.float32, jnp.int32
NT = (((1,), (1,)), ((), ()))

D = 2880
FFW = 1440
TOK = 128
HEAD = 256
COLS = 360
SPAN = 4 * TOK
CAP = 6
DEV = 128
SLICE = 384
PIECES = 8
WIDE = SLICE * PIECES
ROWS = PIECES * CAP
BLOCK = 8
BROWS = BLOCK * CAP
GROUP = 32
GROUPS = DEV // GROUP
GROWS = GROUP * CAP
VMEM = 60 * 1024 * 1024


def ahead():
    ctx, exp = lax.axis_index("ctx"), lax.axis_index("exp")
    z, y = lax.div(ctx, 4), lax.rem(ctx, 4)
    x, core = lax.div(exp, 2), lax.rem(exp, 2)
    zs = [lax.rem(z + step, 4) for step in range(4)]
    ys = [lax.rem(y + step, 4) for step in range(4)]
    xs = [lax.rem(x + step, 4) for step in range(4)]
    cores = [core, 1 - core]
    return zs, ys, xs, cores


def project_kernel(
    attention, weight, out, heads, wide, partial, landed,
    own_sems, head_sems, wide_sems, half_sems, part_sems, relay_sems, send_sems,
):
    zs, ys, xs, cores = ahead()

    def device(dz=0, dy=0, dx=0, dc=0):
        return zs[dz] * 4 + ys[dy], xs[dx] * 2 + cores[dc]

    def lanes(dz, start=0, count=HEAD):
        return pl.ds(dz * HEAD + start, count)

    def remote(source, target, send, receive, **offset):
        pltpu.make_async_remote_copy(
            src_ref=source, dst_ref=target, send_sem=send_sems.at[send], recv_sem=receive,
            device_id=device(**offset), device_id_type=MESH,
        ).start()

    def arrival(target, semaphore):
        pltpu.make_async_copy(target, target, semaphore).wait()

    own_heads = attention.at[pl.ds(pl.multiple_of(zs[0] * SPAN, SPAN), SPAN)]
    own = [
        pltpu.make_async_copy(weight, wide.at[0, :, lanes(0)], own_sems.at[0]),
        pltpu.make_async_copy(own_heads, heads.at[:, lanes(0)], own_sems.at[1]),
    ]
    for copy in own:
        copy.start()
    barrier = pltpu.get_barrier_semaphore()
    friends = (
        [dict(dz=d) for d in (1, 2, 3)] + [dict(dy=d) for d in (1, 2, 3)]
        + [dict(dx=1), dict(dx=3), dict(dc=1)]
    )
    for offset in friends:
        pl.semaphore_signal(barrier, inc=1, device_id=device(**offset), device_id_type=MESH)
    pl.semaphore_wait(barrier, len(friends))

    for dz in (1, 3, 2):
        remote(weight, wide.at[0, :, lanes(dz)], 0, wide_sems.at[dz, 0], dz=dz)
    for dz in (1, 3, 2):
        block = attention.at[pl.ds(pl.multiple_of(zs[dz] * SPAN, SPAN), SPAN)]
        remote(block, heads.at[:, lanes(dz)], 1, head_sems.at[dz], dz=dz)

    def across(dz, dx):
        slot = wide.at[2 * dx, :, lanes(dz)]
        remote(slot, wide.at[2 * dx + 1, :, lanes(dz)], 2, wide_sems.at[dz, 2 * dx + 1], dc=1)

    def sideways(dz):
        slot = wide.at[0, :, lanes(dz)]
        if dz:
            arrival(slot, wide_sems.at[dz, 0])
        else:
            own[0].wait()
        for dx in (1, 3):
            remote(slot, wide.at[2 * dx, :, lanes(dz)], 3, wide_sems.at[dz, 2 * dx], dx=dx)
        across(dz, 0)

    def relay(dz):
        for dx, start, semaphore in ((1, 0, wide_sems.at[dz, 4]), (3, 128, half_sems.at[dz])):
            arrival(wide.at[2 * dx, :, lanes(dz)], wide_sems.at[dz, 2 * dx])
            remote(
                wide.at[2 * dx, :, lanes(dz, start, 128)], wide.at[4, :, lanes(dz, start, 128)],
                4, semaphore, dx=dx,
            )
            across(dz, dx)

    def far(dz):
        arrival(wide.at[4, :, lanes(dz, 0, 128)], wide_sems.at[dz, 4])
        arrival(wide.at[4, :, lanes(dz, 128, 128)], half_sems.at[dz])
        across(dz, 2)

    def column(group):
        return xs[(4 - group // 2) % 4] * 2 + cores[group % 2]

    pending = []

    def multiply(group):
        if group % 2:
            for dz in range(4):
                arrival(wide.at[group, :, lanes(dz)], wide_sems.at[dz, group])
        product = lax.dot_general(
            wide[group], heads[...], NT, preferred_element_type=F32
        ).astype(BF16)
        for block in range(4):
            partial[group, block] = product[:, block * TOK : (block + 1) * TOK]
        for dy in (1, 3, 2):
            remote(
                partial.at[group, ys[dy]], landed.at[dy - 1, group], 5, part_sems.at[dy - 1, group], dy=dy
            )

    def collect(group):
        total = partial[group, ys[0]].astype(F32)
        for dy in (1, 2, 3):
            arrival(landed.at[dy - 1, group], part_sems.at[dy - 1, group])
            total = total + landed[dy - 1, group].astype(F32)
        out[column(group)] = total.astype(BF16)

    sideways(0)
    sideways(1)
    relay(0)
    sideways(3)
    relay(1)
    sideways(2)
    relay(3)
    own[1].wait()
    for dz in (1, 3, 2):
        arrival(heads.at[:, lanes(dz)], head_sems.at[dz])
    multiply(0)
    multiply(1)
    relay(2)
    multiply(2)
    multiply(6)
    far(0)
    far(1)
    multiply(3)
    multiply(7)
    far(3)
    far(2)
    multiply(4)
    collect(0)
    collect(1)
    multiply(5)
    for group in (2, 6, 3, 7, 4, 5):
        collect(group)

    for index, sent in enumerate((
        wide.at[0, :, pl.ds(0, 3 * HEAD)],
        heads.at[:, pl.ds(0, 3 * HEAD)],
        wide.at[pl.ds(0, 4)],
        wide.at[pl.ds(0, 2)],
        wide.at[0],
        landed,
    )):
        arrival(sent, send_sems.at[index])


def project(attention, out_weight):
    anywhere = pl.BlockSpec(memory_space=pl.ANY)
    return pl.pallas_call(
        project_kernel,
        out_shape=jax.ShapeDtypeStruct((8, COLS, TOK), BF16),
        in_specs=[anywhere] * 2,
        out_specs=pl.BlockSpec(memory_space=pltpu.VMEM),
        scratch_shapes=[
            pltpu.VMEM((SPAN, 4 * HEAD), BF16),
            pltpu.VMEM((8, COLS, 4 * HEAD), BF16),
            pltpu.VMEM((8, 4, COLS, TOK), BF16),
            pltpu.VMEM((3, 8, COLS, TOK), BF16),
            pltpu.SemaphoreType.DMA((2,)),
            pltpu.SemaphoreType.DMA((4,)),
            pltpu.SemaphoreType.DMA((4, 8)),
            pltpu.SemaphoreType.DMA((4,)),
            pltpu.SemaphoreType.DMA((3, 8)),
            pltpu.SemaphoreType.DMA((4,)),
            pltpu.SemaphoreType.DMA((6,)),
        ],
        compiler_params=pltpu.CompilerParams(
            vmem_limit_bytes=VMEM, collective_id=1, has_side_effects=True
        ),
    )(attention[0], jnp.swapaxes(out_weight, 0, 1))

def unpack(mixer, messages):
    flat = messages.reshape(BLOCK * ROWS, SLICE)
    sorted_rows = jnp.dot(mixer, flat, preferred_element_type=F32).astype(BF16)
    return [sorted_rows[piece * BROWS : (piece + 1) * BROWS] for piece in range(PIECES)]


def pack(mixer_t, rows):
    stacked = jnp.concatenate(
        [rows[:, piece * SLICE : (piece + 1) * SLICE] for piece in range(PIECES)], axis=0
    )
    mixed = jnp.dot(mixer_t, stacked, preferred_element_type=F32).astype(BF16)
    return mixed.reshape(BLOCK, ROWS, SLICE)


def mixers():
    count = BLOCK * ROWS
    place = jnp.arange(count, dtype=I32)
    piece, position, message = place // BROWS, (place // BLOCK) % CAP, place % BLOCK
    source = message * ROWS + piece * CAP + position
    mixer = (source[:, None] == place[None, :]).astype(BF16)
    mixer_t = (place[:, None] == source[None, :]).astype(BF16)
    return mixer, mixer_t


def slot_columns():
    column = jnp.arange(DEV * CAP, dtype=I32)
    block, position, message = column // BROWS, (column // BLOCK) % CAP, column % BLOCK
    slot = block * BLOCK + message
    group, rest = slot // GROUP, slot % GROUP
    dz, dy, dc = rest // 8, (rest // 2) % 4, rest % 2
    dx = (group + 8 - dz - dy) % 4
    ctx, exp = lax.axis_index("ctx"), lax.axis_index("exp")
    ctx = (ctx // 4 + dz) % 4 * 4 + (ctx % 4 + dy) % 4
    exp = (exp // 2 + dx) % 4 * 2 + (exp % 2 + dc) % 2
    shape = (GROUPS, 1, GROWS)
    return (ctx * 8 + exp).astype(I32).reshape(shape), position.reshape(shape)


def pieces():
    return [(start, min(start + SLICE, D)) for start in range(0, D, SLICE)]


def moe_kernel(
    projected, gain, routes, gate_fixed, expert_col, position_col, mixer, mixer_t,
    w_gate, w_up, w_down,
    out,
    gate, up, down, send, landed, returned, arrived, activated, outputs, normed,
    chooser, shares, totals,
    weight_sems, send_sem, land_sems, result_sem, return_sems,
):
    loads = [
        pltpu.make_async_copy(source.at[0], target, weight_sems.at[i])
        for i, (source, target) in enumerate(((w_gate, gate), (w_up, up), (w_down, down)))
    ]
    for load in loads:
        load.start()
    zs, ys, xs, cores = ahead()

    def each(group, back, act):
        shift = 4 - group if back else group + 4
        across = [lax.rem(xs[0] + shift + (step if back else 4 - step), 4) for step in range(4)]
        for dz in range(4):
            for dy in range(4):
                for dc in range(2):
                    z, y = (zs[-dz % 4], ys[-dy % 4]) if back else (zs[dz], ys[dy])
                    target = (z * 4 + y, across[(dz + dy) % 4] * 2 + cores[dc])
                    slot = group * GROUP + dz * 8 + dy * 2 + dc
                    if dz + dy + dc:
                        act(slot, target)
                    else:
                        pl.when(group > 0)(lambda: act(slot, target))

    barrier = pltpu.get_barrier_semaphore()

    @pl.loop(0, GROUPS)
    def _(group):
        each(group, False, lambda slot, target: pl.semaphore_signal(
            barrier, inc=1, device_id=target, device_id_type=MESH))

    squares = jnp.zeros((1, TOK), F32)
    for start, stop in pieces():
        widened = projected[start:stop, :].astype(F32)
        squares = squares + jnp.sum(widened * widened, axis=0, keepdims=True)
    scale = lax.rsqrt(squares / D + 1e-05)
    normed[:, D:] = jnp.zeros((TOK, WIDE - D), BF16)
    outputs[:, D:] = jnp.zeros((GROWS, WIDE - D), BF16)
    for start, stop in pieces():
        scaled = jnp.transpose(projected[start:stop, :].astype(F32) * scale)
        normed[:, start:stop] = (scaled * gain[:, start:stop]).astype(BF16)
    earlier = lax.broadcasted_iota(I32, (TOK, TOK), 1) < lax.broadcasted_iota(I32, (TOK, TOK), 0)
    earlier = jnp.where(earlier, 1.0, 0.0).astype(BF16)

    @pl.loop(0, GROUPS)
    def _(group):
        fixed = jnp.zeros((TOK, GROWS), I32)
        for k in range(4):
            named = routes[:, k : k + 1] == expert_col[group]
            fixed = fixed + jnp.where(named, gate_fixed[:, k : k + 1], 0)
        chosen = jnp.where(fixed > 0, 1.0, 0.0)
        rank = jnp.dot(earlier, chosen.astype(BF16), preferred_element_type=F32)
        mask = (fixed > 0) & (rank == position_col[group].astype(F32))
        fixed = jnp.where(mask, fixed, 0)
        shares[group, :TOK] = (fixed >> 8).astype(F32).astype(BF16)
        shares[group, TOK:] = (fixed & 255).astype(F32).astype(BF16)
        chooser[group] = jnp.transpose(jnp.where(mask, 1.0, 0.0)).astype(BF16)

    pl.semaphore_wait(barrier, DEV - 1)

    def block_rows(block):
        return pl.ds(pl.multiple_of(block * BROWS, BROWS), BROWS)

    @pl.loop(0, GROUPS)
    def _(group):
        first = group * GROUP
        for piece in range(PIECES):
            columns = pl.ds(piece * SLICE, SLICE)
            arrived[:, columns] = jnp.dot(
                chooser[group], normed[:, columns], preferred_element_type=F32
            ).astype(BF16)

        @pl.loop(0, GROUP // BLOCK)
        def _(block):
            send[pl.ds(first + block * BLOCK, BLOCK)] = pack(mixer_t[...], arrived[block_rows(block), :])

        @pl.when(group == 0)
        def _():
            pltpu.make_async_copy(send.at[0], landed.at[0], land_sems.at[0]).start()

        each(group, False, lambda slot, target: pltpu.make_async_remote_copy(
            src_ref=send.at[slot], dst_ref=landed.at[slot], send_sem=send_sem,
            recv_sem=land_sems.at[group], device_id=target, device_id_type=MESH,
        ).start())

    for load in loads:
        load.wait()

    @pl.loop(0, GROUPS)
    def _(group):
        first = group * GROUP
        span = landed.at[pl.ds(first, GROUP)]
        pltpu.make_async_copy(span, span, land_sems.at[group]).wait()

        @pl.loop(0, GROUP // BLOCK)
        def _(block):
            rows = unpack(mixer[...], landed[pl.ds(first + block * BLOCK, BLOCK)])
            for piece in range(PIECES):
                arrived[block_rows(block), piece * SLICE : (piece + 1) * SLICE] = rows[piece]

        def hidden(start, count):
            units = pl.ds(start, count)
            gate_value = lax.dot_general(arrived[:, :D], gate[units, :], NT, preferred_element_type=F32)
            up_value = lax.dot_general(arrived[:, :D], up[units, :], NT, preferred_element_type=F32)
            activated[:, units] = (
                gate_value / (1.0 + jnp.exp(-1.702 * gate_value)) * (up_value + 1.0)
            ).astype(BF16)

        @pl.loop(0, FFW // 256)
        def _(tile):
            hidden(pl.multiple_of(tile * 256, 256), 256)

        hidden(FFW // 256 * 256, FFW % 256)

        def result(start, count):
            columns = pl.ds(start, count)
            outputs[:, columns] = jnp.dot(
                activated[...], down[:, columns], preferred_element_type=F32
            ).astype(BF16)

        @pl.loop(0, D // 256)
        def _(tile):
            result(pl.multiple_of(tile * 256, 256), 256)

        result(D // 256 * 256, D % 256)

        @pl.loop(0, GROUP // BLOCK)
        def _(block):
            landed[pl.ds(first + block * BLOCK, BLOCK)] = pack(mixer_t[...], outputs[block_rows(block), :])

        @pl.when(group == 0)
        def _():
            pltpu.make_async_copy(landed.at[0], returned.at[0], return_sems.at[0]).start()

        each(group, True, lambda slot, target: pltpu.make_async_remote_copy(
            src_ref=landed.at[slot], dst_ref=returned.at[slot], send_sem=result_sem,
            recv_sem=return_sems.at[group], device_id=target, device_id_type=MESH,
        ).start())

    totals[...] = jnp.zeros(totals.shape, F32)

    @pl.loop(0, GROUPS)
    def _(group):
        first = group * GROUP
        span = returned.at[pl.ds(first, GROUP)]
        pltpu.make_async_copy(span, span, return_sems.at[group]).wait()

        @pl.loop(0, GROUP // BLOCK)
        def _(block):
            rows = unpack(mixer[...], returned[pl.ds(first + block * BLOCK, BLOCK)])
            for piece in range(PIECES):
                arrived[block_rows(block), piece * SLICE : (piece + 1) * SLICE] = rows[piece]

        for start, stop in pieces():
            totals[:, start:stop] += jnp.dot(
                shares[group], arrived[:, start:stop], preferred_element_type=F32
            )

    for start, stop in pieces():
        combined = totals[:TOK, start:stop] * (1.0 / 256.0) + totals[TOK:, start:stop] * (1.0 / 65536.0)
        layer_out = projected[start:stop, :].astype(F32) + jnp.transpose(combined)
        out[start:stop, :] = layer_out.astype(BF16)

    sent = returned.at[pl.ds(1, DEV - 1)]
    pltpu.make_async_copy(sent, sent, send_sem).wait()
    pltpu.make_async_copy(sent, sent, result_sem).wait()


def moe(projected, gain, routes, gate_fixed, w_gate, w_up, w_down):
    near, anywhere = pl.BlockSpec(memory_space=pltpu.VMEM), pl.BlockSpec(memory_space=pl.ANY)
    message = pltpu.VMEM((DEV, ROWS, SLICE), BF16)
    return pl.pallas_call(
        moe_kernel,
        out_shape=jax.ShapeDtypeStruct((D, TOK), BF16),
        in_specs=[near] * 8 + [anywhere] * 3,
        out_specs=near,
        scratch_shapes=[
            pltpu.VMEM((FFW, D), BF16),
            pltpu.VMEM((FFW, D), BF16),
            pltpu.VMEM((FFW, D), BF16),
            message,
            message,
            message,
            pltpu.VMEM((GROWS, WIDE), BF16),
            pltpu.VMEM((GROWS, FFW), BF16),
            pltpu.VMEM((GROWS, WIDE), BF16),
            pltpu.VMEM((TOK, WIDE), BF16),
            pltpu.VMEM((GROUPS, GROWS, TOK), BF16),
            pltpu.VMEM((GROUPS, 2 * TOK, GROWS), BF16),
            pltpu.VMEM((2 * TOK, D), F32),
            pltpu.SemaphoreType.DMA((3,)),
            pltpu.SemaphoreType.DMA,
            pltpu.SemaphoreType.DMA((GROUPS,)),
            pltpu.SemaphoreType.DMA,
            pltpu.SemaphoreType.DMA((GROUPS,)),
        ],
        compiler_params=pltpu.CompilerParams(
            vmem_limit_bytes=VMEM, collective_id=0, has_side_effects=True
        ),
    )(
        projected, gain.reshape(1, D), routes, gate_fixed, *slot_columns(), *mixers(),
        jnp.swapaxes(w_gate, 1, 2), jnp.swapaxes(w_up, 1, 2), w_down,
    )


def shards(attention, out_weight, norm_gain, w_gate, w_up, w_down, routes, gate_fixed):
    projected = project(attention, out_weight).reshape(D, TOK)
    layer_out = moe(projected, norm_gain, routes[0], gate_fixed[0], w_gate, w_up, w_down)
    return jnp.swapaxes(layer_out, 0, 1)[None]


def solution(mesh):
    in_specs = (
        P("exp", None, "ctx"),
        P("ctx", "exp"),
        P(),
        P(("ctx", "exp"), None, None),
        P(("ctx", "exp"), None, None),
        P(("ctx", "exp"), None, None),
        P("exp", "ctx", None),
        P("exp", "ctx", None),
    )
    out_specs = P("exp", "ctx", None)
    return jax.shard_map(shards, mesh=mesh, in_specs=in_specs, out_specs=out_specs, check_vma=False)
```

time: 516 us -> 218 us (0.42)
  waiting for transfers between devices: 243 us -> 0 us
  Pallas kernels: 0 us -> 206 us
  blocking collectives: 81.2 us -> 0 us
  local copies, waits for them, and re-layouts: 77.7 us -> 6.14 us
  matrix products: 59.6 us -> 0 us
  other arithmetic: 21.1 us -> 1.73 us
  between operations: 13.8 us -> 0.02 us
  starting transfers between devices: 12.7 us -> 0 us
    pallas_call x0 -> x2, Pallas kernels: none -> 206 us  [the longest x1 143 us: moe(): pl.pallas_call(moe_kernel, out_shape=jax.ShapeDtypeStruct((D, TOK), BF16)...]
    all_gather x2 -> x0, waiting for transfers between devices: 146 us -> none  [the longest x1 117 us: shards(): lax.all_gather(wide_rows, 'ctx', axis=0, tiled=True)]
    all_to_all x2 -> x0, waiting for transfers between devices: 96 us -> none  [the longest x1 72.3 us: shards(): lax.all_to_all(results, ('ctx', 'exp'), split_axis=0, concat_axis=0, tile...]
    all_to_all x1 -> x0, blocking collectives: 81.2 us -> none  [shards(): lax.all_to_all(outgoing.reshape(device_count, capacity, width), ('ctx', '...]
    dot_general x3 -> x0, matrix products: 59.6 us -> none  [the longest x1 36 us: shards(): jnp.dot(activated, w_down[0], preferred_element_type=jnp.float32)]
    reshape x4 -> x1, local copies, waits for them, and re-layouts: 31.5 us -> 1.31 us  [moe(): gain.reshape(1, D)]
    scatter x1 -> x0, local copies, waits for them, and re-layouts: 16.8 us -> none  [shards(): outgoing = jnp.zeros((device_count * capacity, width), jnp.bfloat16).at[s...]
    all_to_all x2 -> x0, starting transfers between devices: 12.6 us -> none  [the longest x1 6.7 us: shards(): lax.all_to_all(attention, 'ctx', split_axis=1, concat_axis=2, tiled=True)]
  transfers between devices with their start and end apart: 4 -> 0, of which waited for: 4 -> 0; matrix products, arithmetic and copies ran while one was open for 4% -> 0% of each run, Pallas kernels for 0% -> 0%
where the time goes in v2:
time: 218 us; the launch traced here: 214 us
  Pallas kernels  206 us (94%)
  local copies, waits for them, and re-layouts  6.14 us (3%)
    pallas_call x1, Pallas kernels, moe(): pl.pallas_call(moe_kernel, out_shape=jax.ShapeDtypeStruct((D, TOK), BF16)...  143 us
    pallas_call x1, Pallas kernels, project(): pl.pallas_call(project_kernel, out_shape=jax.ShapeDtypeStruct((8, COLS, T...  62.6 us
    unnamed x3, local copies, waits for them, and re-layouts  4.83 us

profile of v2, /device:TPU:1, one launch (start us, length us, event | category | flops | bytes accessed | tf_op | source)
XLA Modules:
  0.0 213.6 jit_solution(7135916851720343287)
XLA Ops:
  0.0 0.8 and_select_fusion
  0.8 1.3 reshape.609.gain
  2.1 1.4 copy.9
  3.5 1.4 copy.10
  4.9 0.9 fusion.1
  5.8 62.6 %shard_map.82 = bf16[8,360,128]{2,1,0:T(8,128)(2,1)} custom-call(bf16[2048,256]{1,0:T(8,128)(2,1)} %bitcast.14, bf16[360,256]{1,0:T(8,128)(2,1)} %bitcast.17), custom_call_target="tpu_custom_call" | custom-call | tf_op jit(solution)/shard_map/pallas_call | solution.py:181
  68.4 143.1 %shard_map.83 = bf16[2880,128]{1,0:T(8,128)(2,1)} custom-call(bf16[2880,128]{1,0:T(8,128)(2,1)} %bitcast.13, f32[1,2880]{1,0:T(1,128)} %reshape.609.gain, s32[128,4]{1,0:T(8,128)} %bitcast.15, s32[128,4]{1,0:T(8,128)} %bitcast.16, s32[4,1,192]{2,1,0:T(1,128)} %get-tuple-element.8.expert_col, s32[4,1,192]{2,1,0:T(1,128)} %get-tuple-element.7.position_col, ...), custom_call_target="tpu_custom_call" | custom-call | tf_op jit(solution)/shard_map/pallas_call | solution.py:423
  211.6 2.0 copy.12
  (1 shorter events, 0.0 us)

commit v3 on v2

--- a/solution.py
+++ b/solution.py
@@ -41,8 +41,8 @@
 
 
 def project_kernel(
-    attention, weight, out, heads, wide, partial, landed,
-    own_sems, head_sems, wide_sems, half_sems, part_sems, relay_sems, send_sems,
+    attention, weight, out, heads, wide, partial, landed, hop,
+    own_sems, head_sems, wide_sems, half_sems, part_sems, hop_sems, send_sems,
 ):
     zs, ys, xs, cores = ahead()
 
@@ -61,16 +61,21 @@
     def arrival(target, semaphore):
         pltpu.make_async_copy(target, target, semaphore).wait()
 
-    own_heads = attention.at[pl.ds(pl.multiple_of(zs[0] * SPAN, SPAN), SPAN)]
+    def tokens(dz, dy):
+        return attention.at[pl.ds(pl.multiple_of(zs[dz] * SPAN + ys[dy] * TOK, TOK), TOK)]
+
+    def head_block(dz, dy):
+        return heads.at[pl.ds(dy * TOK, TOK), lanes(dz)]
+
+    own = [pltpu.make_async_copy(weight, wide.at[0, :, lanes(0)], own_sems.at[4])]
     own = [
-        pltpu.make_async_copy(weight, wide.at[0, :, lanes(0)], own_sems.at[0]),
-        pltpu.make_async_copy(own_heads, heads.at[:, lanes(0)], own_sems.at[1]),
-    ]
+        pltpu.make_async_copy(tokens(0, dy), head_block(0, dy), own_sems.at[dy]) for dy in range(4)
+    ] + own
     for copy in own:
         copy.start()
     barrier = pltpu.get_barrier_semaphore()
     friends = (
-        [dict(dz=d) for d in (1, 2, 3)] + [dict(dy=d) for d in (1, 2, 3)]
+        [dict(dz=d) for d in (1, 2, 3)] + [dict(dy=d) for d in (1, 3)]
         + [dict(dx=1), dict(dx=3), dict(dc=1)]
     )
     for offset in friends:
@@ -79,9 +84,6 @@
 
     for dz in (1, 3, 2):
         remote(weight, wide.at[0, :, lanes(dz)], 0, wide_sems.at[dz, 0], dz=dz)
-    for dz in (1, 3, 2):
-        block = attention.at[pl.ds(pl.multiple_of(zs[dz] * SPAN, SPAN), SPAN)]
-        remote(block, heads.at[:, lanes(dz)], 1, head_sems.at[dz], dz=dz)
 
     def across(dz, dx):
         slot = wide.at[2 * dx, :, lanes(dz)]
@@ -92,7 +94,7 @@
         if dz:
             arrival(slot, wide_sems.at[dz, 0])
         else:
-            own[0].wait()
+            own[4].wait()
         for dx in (1, 3):
             remote(slot, wide.at[2 * dx, :, lanes(dz)], 3, wide_sems.at[dz, 2 * dx], dx=dx)
         across(dz, 0)
@@ -111,58 +113,92 @@
         arrival(wide.at[4, :, lanes(dz, 128, 128)], half_sems.at[dz])
         across(dz, 2)
 
-    def column(group):
-        return xs[(4 - group // 2) % 4] * 2 + cores[group % 2]
-
-    pending = []
-
-    def multiply(group):
+    def ready(group):
         if group % 2:
             for dz in range(4):
                 arrival(wide.at[group, :, lanes(dz)], wide_sems.at[dz, group])
-        product = lax.dot_general(
-            wide[group], heads[...], NT, preferred_element_type=F32
-        ).astype(BF16)
-        for block in range(4):
-            partial[group, block] = product[:, block * TOK : (block + 1) * TOK]
-        for dy in (1, 3, 2):
-            remote(
-                partial.at[group, ys[dy]], landed.at[dy - 1, group], 5, part_sems.at[dy - 1, group], dy=dy
-            )
+
+    def ready_heads(dy):
+        own[dy].wait()
+        for dz in (1, 3, 2):
+            arrival(head_block(dz, dy), head_sems.at[dz, dy])
+
+    def multiply(group, blocks):
+        rows = heads[blocks[0] * TOK : (blocks[-1] + 1) * TOK, :]
+        product = lax.dot_general(wide[group], rows, NT, preferred_element_type=F32).astype(BF16)
+        for place, dy in enumerate(blocks):
+            partial[group, dy] = product[:, place * TOK : (place + 1) * TOK]
+
+    def via(group):
+        return 3 if group % 2 else 1
+
+    def send_hop(group):
+        remote(partial.at[group, 2], hop.at[group], 5, hop_sems.at[group], dy=via(group))
+
+    def send_plain(group):
+        dy = 4 - via(group)
+        remote(partial.at[group, dy], landed.at[dy // 2, group], 5, part_sems.at[dy // 2, group], dy=dy)
+
+    def send_joined(group):
+        dy = via(group)
+        arrival(hop.at[group], hop_sems.at[group])
+        partial[group, dy] = (partial[group, dy].astype(F32) + hop[group].astype(F32)).astype(BF16)
+        remote(partial.at[group, dy], landed.at[dy // 2, group], 5, part_sems.at[dy // 2, group], dy=dy)
 
     def collect(group):
-        total = partial[group, ys[0]].astype(F32)
-        for dy in (1, 2, 3):
-            arrival(landed.at[dy - 1, group], part_sems.at[dy - 1, group])
-            total = total + landed[dy - 1, group].astype(F32)
-        out[column(group)] = total.astype(BF16)
+        total = partial[group, 0].astype(F32)
+        for side in range(2):
+            arrival(landed.at[side, group], part_sems.at[side, group])
+            total = total + landed[side, group].astype(F32)
+        out[xs[(4 - group // 2) % 4] * 2 + cores[group % 2]] = total.astype(BF16)
 
     sideways(0)
+    for dy in (2, 3, 1, 0):
+        for dz in (1, 3, 2):
+            remote(tokens(dz, dy), head_block(dz, dy), 1, head_sems.at[dz, dy], dz=dz)
     sideways(1)
     relay(0)
     sideways(3)
     relay(1)
     sideways(2)
+    ready_heads(2)
+    multiply(0, (2,))
+    send_hop(0)
     relay(3)
-    own[1].wait()
-    for dz in (1, 3, 2):
-        arrival(heads.at[:, lanes(dz)], head_sems.at[dz])
-    multiply(0)
-    multiply(1)
+    ready(1)
+    multiply(1, (2,))
+    send_hop(1)
+    ready_heads(3)
+    multiply(0, (3,))
+    send_plain(0)
     relay(2)
-    multiply(2)
-    multiply(6)
-    far(0)
-    far(1)
-    multiply(3)
-    multiply(7)
-    far(3)
-    far(2)
-    multiply(4)
-    collect(0)
-    collect(1)
-    multiply(5)
+    multiply(1, (3,))
+    ready_heads(1)
+    multiply(1, (1,))
+    send_plain(1)
+    multiply(0, (1,))
+    send_joined(0)
+    send_joined(1)
+    ready_heads(0)
+    multiply(0, (0,))
+    multiply(1, (0,))
+    previous = None
     for group in (2, 6, 3, 7, 4, 5):
+        if group == 3:
+            far(0)
+            far(1)
+        if group == 4:
+            far(3)
+            far(2)
+        ready(group)
+        multiply(group, (0, 1, 2, 3))
+        send_hop(group)
+        send_plain(group)
+        if previous is not None:
+            send_joined(previous)
+        previous = group
+    send_joined(previous)
+    for group in (0, 1, 2, 6, 3, 7, 4, 5):
         collect(group)
 
     for index, sent in enumerate((
@@ -171,7 +207,7 @@
         wide.at[pl.ds(0, 4)],
         wide.at[pl.ds(0, 2)],
         wide.at[0],
-        landed,
+        partial.at[:, pl.ds(0, 3)],
     )):
         arrival(sent, send_sems.at[index])
 
@@ -187,13 +223,14 @@
             pltpu.VMEM((SPAN, 4 * HEAD), BF16),
             pltpu.VMEM((8, COLS, 4 * HEAD), BF16),
             pltpu.VMEM((8, 4, COLS, TOK), BF16),
-            pltpu.VMEM((3, 8, COLS, TOK), BF16),
-            pltpu.SemaphoreType.DMA((2,)),
-            pltpu.SemaphoreType.DMA((4,)),
+            pltpu.VMEM((2, 8, COLS, TOK), BF16),
+            pltpu.VMEM((8, COLS, TOK), BF16),
+            pltpu.SemaphoreType.DMA((5,)),
+            pltpu.SemaphoreType.DMA((4, 4)),
             pltpu.SemaphoreType.DMA((4, 8)),
             pltpu.SemaphoreType.DMA((4,)),
-            pltpu.SemaphoreType.DMA((3, 8)),
-            pltpu.SemaphoreType.DMA((4,)),
+            pltpu.SemaphoreType.DMA((2, 8)),
+            pltpu.SemaphoreType.DMA((8,)),
             pltpu.SemaphoreType.DMA((6,)),
         ],
         compiler_params=pltpu.CompilerParams(
@@ -215,28 +252,34 @@
     return mixed.reshape(BLOCK, ROWS, SLICE)
 
 
-def mixers():
+def sixth(value):
+    whole = (value * 43) >> 8
+    return whole, value - 6 * whole
+
+
+def mixed_places(place):
+    piece, position = sixth(place >> 3)
+    return (place & 7) * ROWS + piece * CAP + position
+
+
+def write_mixers(mixer, mixer_t):
     count = BLOCK * ROWS
-    place = jnp.arange(count, dtype=I32)
-    piece, position, message = place // BROWS, (place // BLOCK) % CAP, place % BLOCK
-    source = message * ROWS + piece * CAP + position
-    mixer = (source[:, None] == place[None, :]).astype(BF16)
-    mixer_t = (place[:, None] == source[None, :]).astype(BF16)
-    return mixer, mixer_t
-
-
-def slot_columns():
-    column = jnp.arange(DEV * CAP, dtype=I32)
-    block, position, message = column // BROWS, (column // BLOCK) % CAP, column % BLOCK
-    slot = block * BLOCK + message
-    group, rest = slot // GROUP, slot % GROUP
-    dz, dy, dc = rest // 8, (rest // 2) % 4, rest % 2
-    dx = (group + 8 - dz - dy) % 4
-    ctx, exp = lax.axis_index("ctx"), lax.axis_index("exp")
-    ctx = (ctx // 4 + dz) % 4 * 4 + (ctx % 4 + dy) % 4
-    exp = (exp // 2 + dx) % 4 * 2 + (exp % 2 + dc) % 2
-    shape = (GROUPS, 1, GROWS)
-    return (ctx * 8 + exp).astype(I32).reshape(shape), position.reshape(shape)
+    source = mixed_places(lax.broadcasted_iota(I32, (count, count), 0))
+    place = lax.broadcasted_iota(I32, (count, count), 1)
+    mixer[...] = jnp.where(source == place, 1.0, 0.0).astype(BF16)
+    source = mixed_places(place)
+    place = lax.broadcasted_iota(I32, (count, count), 0)
+    mixer_t[...] = jnp.where(source == place, 1.0, 0.0).astype(BF16)
+
+
+def slot_columns(group, zs, ys, xs, cores):
+    column = lax.broadcasted_iota(I32, (1, GROWS), 1)
+    dz, position = sixth(column >> 3)
+    dy, dc = (column & 7) >> 1, column & 1
+    dx = (group + 8 - dz - dy) & 3
+    z, y = (zs[0] + dz) & 3, (ys[0] + dy) & 3
+    x, core = (xs[0] + dx) & 3, (cores[0] + dc) & 1
+    return (z * 4 + y) * 8 + x * 2 + core, position
 
 
 def pieces():
@@ -244,12 +287,11 @@
 
 
 def moe_kernel(
-    projected, gain, routes, gate_fixed, expert_col, position_col, mixer, mixer_t,
-    w_gate, w_up, w_down,
+    projected, gain, routes, gate_fixed, w_gate, w_up, w_down,
     out,
     gate, up, down, send, landed, returned, arrived, activated, outputs, normed,
-    chooser, shares, totals,
-    weight_sems, send_sem, land_sems, result_sem, return_sems,
+    chooser, shares, totals, mixer, mixer_t,
+    weight_sems, send_sem, land_sems, result_sem, return_sems, round_sems,
 ):
     loads = [
         pltpu.make_async_copy(source.at[0], target, weight_sems.at[i])
@@ -273,12 +315,22 @@
                     else:
                         pl.when(group > 0)(lambda: act(slot, target))
 
+    lines = {
+        "z": [(zs[d] * 4 + ys[0], xs[0] * 2 + cores[0]) for d in (1, 2, 3)],
+        "y": [(zs[0] * 4 + ys[d], xs[0] * 2 + cores[0]) for d in (1, 2, 3)],
+        "x": [(zs[0] * 4 + ys[0], xs[d] * 2 + cores[c]) for d in range(4) for c in range(2) if d + c],
+    }
+
+    def greet(semaphore, line):
+        for target in lines[line]:
+            pl.semaphore_signal(semaphore, inc=1, device_id=target, device_id_type=MESH)
+
     barrier = pltpu.get_barrier_semaphore()
-
-    @pl.loop(0, GROUPS)
-    def _(group):
-        each(group, False, lambda slot, target: pl.semaphore_signal(
-            barrier, inc=1, device_id=target, device_id_type=MESH))
+    for line in lines:
+        greet(barrier, line)
+    write_mixers(mixer, mixer_t)
+    pl.semaphore_wait(barrier, sum(len(line) for line in lines.values()))
+    greet(round_sems.at[0], "y")
 
     squares = jnp.zeros((1, TOK), F32)
     for start, stop in pieces():
@@ -289,25 +341,31 @@
     outputs[:, D:] = jnp.zeros((GROWS, WIDE - D), BF16)
     for start, stop in pieces():
         scaled = jnp.transpose(projected[start:stop, :].astype(F32) * scale)
-        normed[:, start:stop] = (scaled * gain[:, start:stop]).astype(BF16)
+        normed[:, start:stop] = (scaled * gain[start:stop].reshape(1, stop - start)).astype(BF16)
+    pl.semaphore_wait(round_sems.at[0], len(lines["y"]))
+    greet(round_sems.at[1], "x")
     earlier = lax.broadcasted_iota(I32, (TOK, TOK), 1) < lax.broadcasted_iota(I32, (TOK, TOK), 0)
     earlier = jnp.where(earlier, 1.0, 0.0).astype(BF16)
 
+    named_experts = jnp.transpose(routes[...])
+    named_shares = jnp.transpose(gate_fixed[...])
+
     @pl.loop(0, GROUPS)
     def _(group):
+        expert, position = slot_columns(group, zs, ys, xs, cores)
         fixed = jnp.zeros((TOK, GROWS), I32)
         for k in range(4):
-            named = routes[:, k : k + 1] == expert_col[group]
-            fixed = fixed + jnp.where(named, gate_fixed[:, k : k + 1], 0)
+            named = named_experts[:, k : k + 1] == expert
+            fixed = fixed + jnp.where(named, named_shares[:, k : k + 1], 0)
         chosen = jnp.where(fixed > 0, 1.0, 0.0)
         rank = jnp.dot(earlier, chosen.astype(BF16), preferred_element_type=F32)
-        mask = (fixed > 0) & (rank == position_col[group].astype(F32))
+        mask = (fixed > 0) & (rank == position.astype(F32))
         fixed = jnp.where(mask, fixed, 0)
         shares[group, :TOK] = (fixed >> 8).astype(F32).astype(BF16)
         shares[group, TOK:] = (fixed & 255).astype(F32).astype(BF16)
         chooser[group] = jnp.transpose(jnp.where(mask, 1.0, 0.0)).astype(BF16)
 
-    pl.semaphore_wait(barrier, DEV - 1)
+    pl.semaphore_wait(round_sems.at[1], len(lines["x"]))
 
     def block_rows(block):
         return pl.ds(pl.multiple_of(block * BROWS, BROWS), BROWS)
@@ -423,7 +481,7 @@
     return pl.pallas_call(
         moe_kernel,
         out_shape=jax.ShapeDtypeStruct((D, TOK), BF16),
-        in_specs=[near] * 8 + [anywhere] * 3,
+        in_specs=[near] * 4 + [anywhere] * 3,
         out_specs=near,
         scratch_shapes=[
             pltpu.VMEM((FFW, D), BF16),
@@ -439,17 +497,20 @@
             pltpu.VMEM((GROUPS, GROWS, TOK), BF16),
             pltpu.VMEM((GROUPS, 2 * TOK, GROWS), BF16),
             pltpu.VMEM((2 * TOK, D), F32),
+            pltpu.VMEM((BLOCK * ROWS, BLOCK * ROWS), BF16),
+            pltpu.VMEM((BLOCK * ROWS, BLOCK * ROWS), BF16),
             pltpu.SemaphoreType.DMA((3,)),
             pltpu.SemaphoreType.DMA,
             pltpu.SemaphoreType.DMA((GROUPS,)),
             pltpu.SemaphoreType.DMA,
             pltpu.SemaphoreType.DMA((GROUPS,)),
+            pltpu.SemaphoreType.REGULAR((2,)),
         ],
         compiler_params=pltpu.CompilerParams(
             vmem_limit_bytes=VMEM, collective_id=0, has_side_effects=True
         ),
     )(
-        projected, gain.reshape(1, D), routes, gate_fixed, *slot_columns(), *mixers(),
+        projected, gain, jnp.swapaxes(routes, 0, 1), jnp.swapaxes(gate_fixed, 0, 1),
         jnp.swapaxes(w_gate, 1, 2), jnp.swapaxes(w_up, 1, 2), w_down,
     )
 

time: 218 us -> 201 us (0.922); the launches traced: 214 us -> 200 us
  Pallas kernels: 206 us -> 198 us
  local copies, waits for them, and re-layouts: 6.14 us -> 2.03 us
    pallas_call x1, Pallas kernels: 62.6 us -> 58.1 us  [project(): pl.pallas_call(project_kernel, out_shape=jax.ShapeDtypeStruct((8, COLS, T...]
    pallas_call x1, Pallas kernels: 143 us -> 139 us  [moe(): pl.pallas_call(moe_kernel, out_shape=jax.ShapeDtypeStruct((D, TOK), BF16)...]
    unnamed x3 -> x1, local copies, waits for them, and re-layouts: 4.83 us -> 2.03 us
where the time goes in v3:
time: 201 us; the launch traced here: 200 us
  Pallas kernels  198 us (99%)
  local copies, waits for them, and re-layouts  2.03 us (1%)
    pallas_call x1, Pallas kernels, moe(): pl.pallas_call(moe_kernel, out_shape=jax.ShapeDtypeStruct((D, TOK), BF16)...  139 us
    pallas_call x1, Pallas kernels, project(): pl.pallas_call(project_kernel, out_shape=jax.ShapeDtypeStruct((8, COLS, T...  58.1 us

profile of v3, /device:TPU:1, one launch (start us, length us, event | category | flops | bytes accessed | tf_op | source)
XLA Modules:
  0.0 199.6 jit_solution(1897766335179392730)
XLA Ops:
  0.0 58.1 %shard_map.82 = bf16[8,360,128]{2,1,0:T(8,128)(2,1)} custom-call(bf16[2048,256]{1,0:T(8,128)(2,1)} %bitcast.18, bf16[360,256]{1,0:T(8,128)(2,1)} %bitcast.19), custom_call_target="tpu_custom_call" | custom-call | tf_op jit(solution)/shard_map/pallas_call | solution.py:217
  58.1 139.4 %shard_map.83 = bf16[2880,128]{1,0:T(8,128)(2,1)} custom-call(bf16[2880,128]{1,0:T(8,128)(2,1)} %bitcast.17, f32[2880]{0:T(1024)} %gain.1, s32[4,128]{1,0:T(4,128)} %bitcast.20, s32[4,128]{1,0:T(4,128)} %bitcast.21, bf16[1,1440,2880]{2,1,0:T(8,128)(2,1)} %bitcast.14, bf16[1,1440,2880]{2,1,0:T(8,128)(2,1)} %bitcast.15, bf16[1,1440,2880]{2,1,0:T(8,128)(2,1)} %w_down.1), custom_call_target="tpu_custom_call" | custom-call | tf_op jit(solution)/shard_map/pallas_call | solution.py:481
  197.5 2.0 %copy.10 = bf16[1,128,2880]{1,2,0:T(8,128)(2,1)} copy(bf16[1,128,2880]{1,2,0:T(8,128)(2,1)} %bitcast.16) | data formatting | bytes 1474560

commit v4 on v3

v4 whole, which is shorter than its diff:
```python
import jax
import jax.numpy as jnp
import numpy as np
from jax import lax
from jax.experimental import pallas as pl
from jax.experimental.pallas import tpu as pltpu
from jax.sharding import PartitionSpec as P

MESH = pl.DeviceIdType.MESH
BF16, F32, I32 = jnp.bfloat16, jnp.float32, jnp.int32
NT = (((1,), (1,)), ((), ()))

D = 2880
FFW = 1440
TOK = 128
HEAD = 256
COLS = 360
SPAN = 4 * TOK
CAP = 6
DEV = 128
SLICE = 384
PIECES = 8
WIDE = SLICE * PIECES
ROWS = PIECES * CAP
BLOCK = 4
BROWS = BLOCK * CAP
LAYER = 8 // BLOCK
GROUP = 32
GROUPS = DEV // GROUP
GROWS = GROUP * CAP
LAYERS = GROUP // 8


def hops(offset):
    return sum(min(step, 4 - step) for step in offset[:3])


OFFSETS = sorted(
    ((dz, dy, dx, dc) for dz in range(4) for dy in range(4) for dx in range(4) for dc in range(2)),
    key=lambda offset: (hops(offset), (offset[0] * 5 + offset[1] * 3 + offset[2] * 7 + offset[3] * 4) % 11),
)
OWN = OFFSETS.index((0, 0, 0, 0))
VMEM = 62 * 1024 * 1024


def ahead():
    ctx, exp = lax.axis_index("ctx"), lax.axis_index("exp")
    z, y = lax.div(ctx, 4), lax.rem(ctx, 4)
    x, core = lax.div(exp, 2), lax.rem(exp, 2)
    zs = [lax.rem(z + step, 4) for step in range(4)]
    ys = [lax.rem(y + step, 4) for step in range(4)]
    xs = [lax.rem(x + step, 4) for step in range(4)]
    cores = [core, 1 - core]
    return zs, ys, xs, cores


def project(
    place, meanwhile, attention, weight, projected, heads, wide, partial, sums, hop,
    own_sems, head_sems, wide_sems, half_sems, part_sems, hop_sems, send_sems,
):
    zs, ys, xs, cores = place

    def device(dz=0, dy=0, dx=0, dc=0):
        return zs[dz] * 4 + ys[dy], xs[dx] * 2 + cores[dc]

    def lanes(dz, start=0, count=HEAD):
        return pl.ds(dz * HEAD + start, count)

    def remote(source, target, send, receive, **offset):
        pltpu.make_async_remote_copy(
            src_ref=source, dst_ref=target, send_sem=send_sems.at[send], recv_sem=receive,
            device_id=device(**offset), device_id_type=MESH,
        ).start()

    def arrival(target, semaphore):
        pltpu.make_async_copy(target, target, semaphore).wait()

    def tokens(dz, dy):
        return attention.at[pl.ds(pl.multiple_of(zs[dz] * SPAN + ys[dy] * TOK, TOK), TOK)]

    def head_block(dz, dy):
        return heads.at[pl.ds(dy * TOK, TOK), lanes(dz)]

    own = [pltpu.make_async_copy(weight, wide.at[0, :, lanes(0)], own_sems.at[4])]
    own = [
        pltpu.make_async_copy(tokens(0, dy), head_block(0, dy), own_sems.at[dy]) for dy in range(4)
    ] + own
    for copy in own:
        copy.start()
    barrier = pltpu.get_barrier_semaphore()
    friends = (
        [dict(dz=d) for d in (1, 2, 3)] + [dict(dy=d) for d in (1, 3)]
        + [dict(dx=1), dict(dx=3), dict(dc=1)]
    )
    for offset in friends:
        pl.semaphore_signal(barrier, inc=1, device_id=device(**offset), device_id_type=MESH)
    pl.semaphore_wait(barrier, len(friends))

    for dz in (1, 3, 2):
        remote(weight, wide.at[0, :, lanes(dz)], 0, wide_sems.at[dz, 0], dz=dz)

    def across(dz, dx):
        slot = wide.at[2 * dx, :, lanes(dz)]
        remote(slot, wide.at[2 * dx + 1, :, lanes(dz)], 2, wide_sems.at[dz, 2 * dx + 1], dc=1)

    def sideways(dz):
        slot = wide.at[0, :, lanes(dz)]
        if dz:
            arrival(slot, wide_sems.at[dz, 0])
        else:
            own[4].wait()
        for dx in (1, 3):
            remote(slot, wide.at[2 * dx, :, lanes(dz)], 3, wide_sems.at[dz, 2 * dx], dx=dx)
        across(dz, 0)

    def relay(dz):
        for dx, start, semaphore in ((1, 0, wide_sems.at[dz, 4]), (3, 128, half_sems.at[dz])):
            arrival(wide.at[2 * dx, :, lanes(dz)], wide_sems.at[dz, 2 * dx])
            remote(
                wide.at[2 * dx, :, lanes(dz, start, 128)], wide.at[4, :, lanes(dz, start, 128)],
                4, semaphore, dx=dx,
            )
            across(dz, dx)

    def far(dz):
        arrival(wide.at[4, :, lanes(dz, 0, 128)], wide_sems.at[dz, 4])
        arrival(wide.at[4, :, lanes(dz, 128, 128)], half_sems.at[dz])
        across(dz, 2)

    def ready(group):
        if group % 2:
            for dz in range(4):
                arrival(wide.at[group, :, lanes(dz)], wide_sems.at[dz, group])

    def ready_heads(dy):
        own[dy].wait()
        for dz in (1, 3, 2):
            arrival(head_block(dz, dy), head_sems.at[dz, dy])

    def multiply(group, blocks):
        rows = heads[blocks[0] * TOK : (blocks[-1] + 1) * TOK, :]
        product = lax.dot_general(wide[group], rows, NT, preferred_element_type=F32).astype(BF16)
        for place, dy in enumerate(blocks):
            partial[group, dy] = product[:, place * TOK : (place + 1) * TOK]

    def via(group):
        return 3 if group % 2 else 1

    def send_hop(group):
        remote(partial.at[group, 2], hop.at[group], 5, hop_sems.at[group], dy=via(group))

    def send_plain(group):
        dy = 4 - via(group)
        remote(partial.at[group, dy], sums.at[dy // 2, group], 5, part_sems.at[dy // 2, group], dy=dy)

    def send_joined(group):
        dy = via(group)
        arrival(hop.at[group], hop_sems.at[group])
        partial[group, dy] = (partial[group, dy].astype(F32) + hop[group].astype(F32)).astype(BF16)
        remote(partial.at[group, dy], sums.at[dy // 2, group], 5, part_sems.at[dy // 2, group], dy=dy)

    def collect(group):
        total = partial[group, 0].astype(F32)
        for side in range(2):
            arrival(sums.at[side, group], part_sems.at[side, group])
            total = total + sums[side, group].astype(F32)
        total = total.astype(BF16).astype(F32)
        column = xs[(4 - group // 2) % 4] * 2 + cores[group % 2]
        projected[pl.ds(pl.multiple_of(column * COLS, 8), COLS), :] = total
        return jnp.sum(total * total, axis=0, keepdims=True)

    sideways(0)
    for dy in (2, 3, 1, 0):
        for dz in (1, 3, 2):
            remote(tokens(dz, dy), head_block(dz, dy), 1, head_sems.at[dz, dy], dz=dz)
    sideways(1)
    relay(0)
    sideways(3)
    relay(1)
    sideways(2)
    meanwhile()
    ready_heads(2)
    multiply(0, (2,))
    send_hop(0)
    relay(3)
    ready(1)
    multiply(1, (2,))
    send_hop(1)
    ready_heads(3)
    multiply(0, (3,))
    send_plain(0)
    relay(2)
    multiply(1, (3,))
    ready_heads(1)
    multiply(1, (1,))
    send_plain(1)
    multiply(0, (1,))
    send_joined(0)
    send_joined(1)
    ready_heads(0)
    multiply(0, (0,))
    multiply(1, (0,))
    previous = None
    for group in (2, 6, 3, 7, 4, 5):
        if group == 3:
            far(0)
            far(1)
        if group == 4:
            far(3)
            far(2)
        ready(group)
        multiply(group, (0, 1, 2, 3))
        send_hop(group)
        send_plain(group)
        if previous is not None:
            send_joined(previous)
        previous = group
    send_joined(previous)
    squares = jnp.zeros((1, TOK), F32)
    for group in (0, 1, 2, 6, 3, 7, 4, 5):
        squares = squares + collect(group)
    sent = enumerate((
        wide.at[0, :, pl.ds(0, 3 * HEAD)],
        heads.at[:, pl.ds(0, 3 * HEAD)],
        wide.at[pl.ds(0, 4)],
        wide.at[pl.ds(0, 2)],
        wide.at[0],
        partial.at[:, pl.ds(0, 3)],
    ))
    return squares, lambda: [arrival(target, send_sems.at[index]) for index, target in sent]


def unpack(mixer, messages, rows, block):
    flat = messages.reshape(BLOCK * ROWS, SLICE)
    sorted_rows = jnp.dot(mixer, flat, preferred_element_type=F32).astype(BF16)
    for piece in range(PIECES):
        rows[block * BROWS : (block + 1) * BROWS, piece * SLICE : (piece + 1) * SLICE] = sorted_rows[
            piece * BROWS : (piece + 1) * BROWS
        ]


def pack(mixer_t, rows, block):
    stacked = jnp.concatenate(
        [
            rows[block * BROWS : (block + 1) * BROWS, piece * SLICE : (piece + 1) * SLICE]
            for piece in range(PIECES)
        ],
        axis=0,
    )
    mixed = jnp.dot(mixer_t, stacked, preferred_element_type=F32).astype(BF16)
    return mixed.reshape(BLOCK, ROWS, SLICE)


def sixth(value):
    whole = (value * 43) >> 8
    return whole, value - 6 * whole


def mixed_places(place):
    piece, position = sixth(place >> 2)
    return (place & 3) * ROWS + piece * CAP + position


def write_mixers(mixer, mixer_t):
    count = BLOCK * ROWS
    source = mixed_places(lax.broadcasted_iota(I32, (count, count), 0))
    place = lax.broadcasted_iota(I32, (count, count), 1)
    mixer[...] = jnp.where(source == place, 1.0, 0.0).astype(BF16)
    source = mixed_places(place)
    place = lax.broadcasted_iota(I32, (count, count), 0)
    mixer_t[...] = jnp.where(source == place, 1.0, 0.0).astype(BF16)


def slot_columns(offsets, zs, ys, xs, cores):
    position = sixth(lax.broadcasted_iota(I32, (1, GROWS), 1) >> 2)[1]
    dz, dy, dx, dc = offsets >> 5, (offsets >> 3) & 3, (offsets >> 1) & 3, offsets & 1
    z, y = (zs[0] + dz) & 3, (ys[0] + dy) & 3
    x, core = (xs[0] + dx) & 3, (cores[0] + dc) & 1
    return (z * 4 + y) * 8 + x * 2 + core, position


def row_offsets():
    row = np.arange(DEV * CAP)
    slot = row // BROWS * BLOCK + row % BLOCK
    numbers = np.array([dz * 32 + dy * 8 + dx * 2 + dc for dz, dy, dx, dc in OFFSETS], np.int32)
    return jnp.asarray(numbers[slot].reshape(GROUPS, 1, GROWS))


HALF = 1408


def pieces():
    return [(start, min(start + SLICE, D)) for start in range(0, D, SLICE)]


def layer_kernel(
    attention, out_weight, gain, routes, gate_fixed, row_offset, w_gate, w_up, w_down,
    out,
    projected, heads, wide, partial, sums, hop,
    own_sems, head_sems, wide_sems, half_sems, part_sems, hop_sems, part_send_sems,
    gate, up, down, send, landed, returned, arrived, activated, normed,
    chooser, shares, totals, mixer, mixer_t,
    weight_sems, send_sem, land_sems, result_sem, return_sems,
):
    loads = [
        pltpu.make_async_copy(source.at[0], target, weight_sems.at[i])
        for i, (source, target) in enumerate(((w_gate, gate), (w_up, up), (w_down, down)))
    ]
    place = ahead()
    zs, ys, xs, cores = place

    def each(group, back, act, layers=range(LAYERS)):
        sign = -1 if back else 1

        def some(first, count):
            for slot in range(first, first + count):
                dz, dy, dx, dc = OFFSETS[slot]
                if slot != OWN:
                    target = (
                        zs[sign * dz % 4] * 4 + ys[sign * dy % 4],
                        xs[sign * dx % 4] * 2 + cores[dc],
                    )
                    act(slot, target)

        for here in range(GROUPS):
            for layer in layers:
                pl.when(group == here)(lambda: some(here * GROUP + layer * 8, 8))

    def prepare():
        write_mixers(mixer, mixer_t)
        earlier = lax.broadcasted_iota(I32, (TOK, TOK), 1) < lax.broadcasted_iota(I32, (TOK, TOK), 0)
        earlier = jnp.where(earlier, 1.0, 0.0).astype(BF16)

        named_experts = jnp.transpose(routes[...])
        named_shares = jnp.transpose(gate_fixed[...])

        @pl.loop(0, GROUPS)
        def _(group):
            expert, position = slot_columns(row_offset[group], zs, ys, xs, cores)
            fixed = jnp.zeros((TOK, GROWS), I32)
            for k in range(4):
                named = named_experts[:, k : k + 1] == expert
                fixed = fixed + jnp.where(named, named_shares[:, k : k + 1], 0)
            chosen = jnp.where(fixed > 0, 1.0, 0.0)
            rank = jnp.dot(earlier, chosen.astype(BF16), preferred_element_type=F32)
            mask = (fixed > 0) & (rank == position.astype(F32))
            fixed = jnp.where(mask, fixed, 0)
            shares[group, :TOK] = (fixed >> 8).astype(F32).astype(BF16)
            shares[group, TOK:] = (fixed & 255).astype(F32).astype(BF16)
            chooser[group] = jnp.transpose(jnp.where(mask, 1.0, 0.0)).astype(BF16)

    squares, last_waits = project(
        place, prepare, attention, out_weight, projected, heads, wide, partial, sums, hop,
        own_sems, head_sems, wide_sems, half_sems, part_sems, hop_sems, part_send_sems,
    )
    for load in loads:
        load.start()
    scale = lax.rsqrt(squares / D + 1e-05)
    normed[:, D:] = jnp.zeros((TOK, WIDE - D), BF16)
    for start, stop in pieces():
        scaled = jnp.transpose(projected[start:stop, :] * scale)
        normed[:, start:stop] = (scaled * gain[start:stop].reshape(1, stop - start)).astype(BF16)

    @pl.loop(0, GROUPS)
    def _(group):
        first = group * GROUP
        for piece in range(PIECES):
            columns = pl.ds(piece * SLICE, SLICE)
            arrived[:, columns] = jnp.dot(
                chooser[group], normed[:, columns], preferred_element_type=F32
            ).astype(BF16)

        for layer in range(4):
            for block in range(layer * LAYER, layer * LAYER + LAYER):
                send[pl.ds(first + block * BLOCK, BLOCK)] = pack(mixer_t[...], arrived, block)
            if layer == OWN % GROUP // 8:
                @pl.when(group == OWN // GROUP)
                def _():
                    pltpu.make_async_copy(send.at[OWN], landed.at[OWN], land_sems.at[group]).start()

            each(group, False, lambda slot, target: pltpu.make_async_remote_copy(
                src_ref=send.at[slot], dst_ref=landed.at[slot], send_sem=send_sem,
                recv_sem=land_sems.at[group], device_id=target, device_id_type=MESH,
            ).start(), [layer])

    for load in loads:
        load.wait()

    @pl.loop(0, GROUPS)
    def _(group):
        first = group * GROUP
        span = landed.at[pl.ds(first, GROUP)]
        pltpu.make_async_copy(span, span, land_sems.at[group]).wait()

        for block in range(GROUP // BLOCK):
            unpack(mixer[...], landed[pl.ds(first + block * BLOCK, BLOCK)], arrived, block)

        gate_value = lax.dot_general(arrived[:, :D], gate[...], NT, preferred_element_type=F32)
        up_value = lax.dot_general(arrived[:, :D], up[...], NT, preferred_element_type=F32)
        activated[...] = (
            gate_value / (1.0 + jnp.exp(-1.702 * gate_value)) * (up_value + 1.0)
        ).astype(BF16)
        for columns in (slice(0, HALF), slice(HALF, D)):
            arrived[:, columns] = jnp.dot(
                activated[...], down[:, columns], preferred_element_type=F32
            ).astype(BF16)
        for block in range(GROUP // BLOCK):
            landed[pl.ds(first + block * BLOCK, BLOCK)] = pack(mixer_t[...], arrived, block)

        @pl.when(group == OWN // GROUP)
        def _():
            pltpu.make_async_copy(landed.at[OWN], returned.at[OWN], return_sems.at[group]).start()

        each(group, True, lambda slot, target: pltpu.make_async_remote_copy(
            src_ref=landed.at[slot], dst_ref=returned.at[slot], send_sem=result_sem,
            recv_sem=return_sems.at[group], device_id=target, device_id_type=MESH,
        ).start())

    totals[...] = jnp.zeros(totals.shape, F32)

    @pl.loop(0, GROUPS)
    def _(group):
        first = group * GROUP
        span = returned.at[pl.ds(first, GROUP)]
        pltpu.make_async_copy(span, span, return_sems.at[group]).wait()

        for block in range(GROUP // BLOCK):
            unpack(mixer[...], returned[pl.ds(first + block * BLOCK, BLOCK)], arrived, block)

        for start, stop in pieces():
            totals[:, start:stop] += jnp.dot(
                shares[group], arrived[:, start:stop], preferred_element_type=F32
            )

    for start, stop in pieces():
        combined = totals[:TOK, start:stop] * (1.0 / 256.0) + totals[TOK:, start:stop] * (1.0 / 65536.0)
        layer_out = projected[start:stop, :] + jnp.transpose(combined)
        out[start:stop, :] = layer_out.astype(BF16)

    sent = returned.at[pl.ds(1, DEV - 1)]
    pltpu.make_async_copy(sent, sent, send_sem).wait()
    pltpu.make_async_copy(sent, sent, result_sem).wait()
    last_waits()


def shards(attention, out_weight, norm_gain, w_gate, w_up, w_down, routes, gate_fixed):
    near, anywhere = pl.BlockSpec(memory_space=pltpu.VMEM), pl.BlockSpec(memory_space=pl.ANY)
    message = pltpu.VMEM((DEV, ROWS, SLICE), BF16)
    mixer = pltpu.VMEM((BLOCK * ROWS, BLOCK * ROWS), BF16)
    layer_out = pl.pallas_call(
        layer_kernel,
        out_shape=jax.ShapeDtypeStruct((D, TOK), BF16),
        in_specs=[anywhere] * 2 + [near] * 4 + [anywhere] * 3,
        out_specs=near,
        scratch_shapes=[
            pltpu.VMEM((D, TOK), F32),
            pltpu.VMEM((SPAN, 4 * HEAD), BF16),
            pltpu.VMEM((8, COLS, 4 * HEAD), BF16),
            pltpu.VMEM((8, 4, COLS, TOK), BF16),
            pltpu.VMEM((2, 8, COLS, TOK), BF16),
            pltpu.VMEM((8, COLS, TOK), BF16),
            pltpu.SemaphoreType.DMA((5,)),
            pltpu.SemaphoreType.DMA((4, 4)),
            pltpu.SemaphoreType.DMA((4, 8)),
            pltpu.SemaphoreType.DMA((4,)),
            pltpu.SemaphoreType.DMA((2, 8)),
            pltpu.SemaphoreType.DMA((8,)),
            pltpu.SemaphoreType.DMA((6,)),
            pltpu.VMEM((FFW, D), BF16),
            pltpu.VMEM((FFW, D), BF16),
            pltpu.VMEM((FFW, D), BF16),
            message,
            message,
            message,
            pltpu.VMEM((GROWS, WIDE), BF16),
            pltpu.VMEM((GROWS, FFW), BF16),
            pltpu.VMEM((TOK, WIDE), BF16),
            pltpu.VMEM((GROUPS, GROWS, TOK), BF16),
            pltpu.VMEM((GROUPS, 2 * TOK, GROWS), BF16),
            pltpu.VMEM((2 * TOK, D), F32),
            mixer,
            mixer,
            pltpu.SemaphoreType.DMA((3,)),
            pltpu.SemaphoreType.DMA,
            pltpu.SemaphoreType.DMA((GROUPS,)),
            pltpu.SemaphoreType.DMA,
            pltpu.SemaphoreType.DMA((GROUPS,)),
        ],
        compiler_params=pltpu.CompilerParams(
            vmem_limit_bytes=VMEM, collective_id=0, has_side_effects=True
        ),
    )(
        attention[0], jnp.swapaxes(out_weight, 0, 1), norm_gain,
        jnp.swapaxes(routes[0], 0, 1), jnp.swapaxes(gate_fixed[0], 0, 1), row_offsets(),
        jnp.swapaxes(w_gate, 1, 2), jnp.swapaxes(w_up, 1, 2), w_down,
    )
    return jnp.swapaxes(layer_out, 0, 1)[None]


def solution(mesh):
    in_specs = (
        P("exp", None, "ctx"),
        P("ctx", "exp"),
        P(),
        P(("ctx", "exp"), None, None),
        P(("ctx", "exp"), None, None),
        P(("ctx", "exp"), None, None),
        P("exp", "ctx", None),
        P("exp", "ctx", None),
    )
    out_specs = P("exp", "ctx", None)
    return jax.shard_map(shards, mesh=mesh, in_specs=in_specs, out_specs=out_specs, check_vma=False)
```

time: 201 us -> 173 us (0.86)
  Pallas kernels: 198 us -> 171 us
    pallas_call x2 -> x1, Pallas kernels: 198 us -> 171 us  [shards(): pl.pallas_call(layer_kernel, out_shape=jax.ShapeDtypeStruct((D, TOK), BF1...]
where the time goes in v4:
time: 173 us
  Pallas kernels  171 us (99%)
  local copies, waits for them, and re-layouts  2.03 us (1%)
    pallas_call x1, Pallas kernels, shards(): pl.pallas_call(layer_kernel, out_shape=jax.ShapeDtypeStruct((D, TOK), BF1...  171 us

profile of v4, /device:TPU:1, one launch (start us, length us, event | category | flops | bytes accessed | tf_op | source)
XLA Modules:
  0.0 172.6 jit_solution(14401838886026577678)
XLA Ops:
  0.0 170.5 %shard_map.91 = bf16[2880,128]{1,0:T(8,128)(2,1)} custom-call(bf16[2048,256]{1,0:T(8,128)(2,1)} %bitcast.16, bf16[360,256]{1,0:T(8,128)(2,1)} %bitcast.17, f32[2880]{0:T(1024)} %gain.1, s32[4,128]{1,0:T(4,128)} %bitcast.18, s32[4,128]{1,0:T(4,128)} %bitcast.19, s32[4,1,192]{2,1,0:T(1,128)} %constant.2.clone.row_offset, bf16[1,1440,2880]{2,1,0:T(8,128)(2,1)} %bitcast.13, ...), custom_call_target="tpu_custom_call" | custom-call | tf_op jit(solution)/shard_map/pallas_call | solution.py:450
  170.5 2.0 %copy.11 = bf16[1,128,2880]{1,2,0:T(8,128)(2,1)} copy(bf16[1,128,2880]{1,2,0:T(8,128)(2,1)} %bitcast.15) | data formatting | bytes 1474560

commit v5 on v4

--- a/solution.py
+++ b/solution.py
@@ -35,9 +35,13 @@
     return sum(min(step, 4 - step) for step in offset[:3])
 
 
+def spread(offset):
+    return (offset[0] * 5 + offset[1] * 3 + offset[2] * 7 + offset[3] * 4) % 11
+
+
 OFFSETS = sorted(
     ((dz, dy, dx, dc) for dz in range(4) for dy in range(4) for dx in range(4) for dc in range(2)),
-    key=lambda offset: (hops(offset), (offset[0] * 5 + offset[1] * 3 + offset[2] * 7 + offset[3] * 4) % 11),
+    key=lambda offset: (hops(offset), spread(offset) * 7 % 11, offset),
 )
 OWN = OFFSETS.index((0, 0, 0, 0))
 VMEM = 62 * 1024 * 1024
@@ -169,17 +173,22 @@
         projected[pl.ds(pl.multiple_of(column * COLS, 8), COLS), :] = total
         return jnp.sum(total * total, axis=0, keepdims=True)
 
-    sideways(0)
-    for dy in (2, 3, 1, 0):
+    def send_heads(dy):
         for dz in (1, 3, 2):
             remote(tokens(dz, dy), head_block(dz, dy), 1, head_sems.at[dz, dy], dz=dz)
+
+    sideways(0)
     sideways(1)
+    sideways(3)
+    send_heads(2)
     relay(0)
-    sideways(3)
+    sideways(2)
+    send_heads(3)
+    send_heads(1)
     relay(1)
-    sideways(2)
     meanwhile()
     ready_heads(2)
+    send_heads(0)
     multiply(0, (2,))
     send_hop(0)
     relay(3)

time: 173 us -> 170 us (0.983)
  Pallas kernels: 171 us -> 167 us
    pallas_call x1, Pallas kernels: 171 us -> 167 us  [shards(): pl.pallas_call(layer_kernel, out_shape=jax.ShapeDtypeStruct((D, TOK), BF1...]
where the time goes in v5:
time: 170 us; the launch traced here: 169 us
  Pallas kernels  167 us (98%)
  local copies, waits for them, and re-layouts  2.03 us (1%)
    pallas_call x1, Pallas kernels, shards(): pl.pallas_call(layer_kernel, out_shape=jax.ShapeDtypeStruct((D, TOK), BF1...  167 us

profile of v5, /device:TPU:1, one launch (start us, length us, event | category | flops | bytes accessed | tf_op | source)
XLA Modules:
  0.0 169.0 jit_solution(17806981744826017642)
XLA Ops:
  0.0 166.9 %shard_map.91 = bf16[2880,128]{1,0:T(8,128)(2,1)} custom-call(bf16[2048,256]{1,0:T(8,128)(2,1)} %bitcast.16, bf16[360,256]{1,0:T(8,128)(2,1)} %bitcast.17, f32[2880]{0:T(1024)} %gain.1, s32[4,128]{1,0:T(4,128)} %bitcast.18, s32[4,128]{1,0:T(4,128)} %bitcast.19, s32[4,1,192]{2,1,0:T(1,128)} %constant.2.clone.row_offset, bf16[1,1440,2880]{2,1,0:T(8,128)(2,1)} %bitcast.13, ...), custom_call_target="tpu_custom_call" | custom-call | tf_op jit(solution)/shard_map/pallas_call | solution.py:459
  166.9 2.0 %copy.11 = bf16[1,128,2880]{1,2,0:T(8,128)(2,1)} copy(bf16[1,128,2880]{1,2,0:T(8,128)(2,1)} %bitcast.15) | data formatting | bytes 1474560
